TPU v7x, 32 devices: a whole 2x2x4 slice. The times are simulated.
32 devices in a mesh: groups: 2 (over y), weight: 4 (over x, core), dp: 4 (over z).
Axes of the slice: x: 2, y: 2, z: 4, core: 2. Of those that a mesh axis runs over, the one named last changes fastest.
Arguments:
- tokens: bfloat16 [4, 64, 4096], P('weight', ('groups', 'dp')), parts along dimension 1, may hold values from -6 to 6
- gate_blocks: bfloat16 [1792, 128, 128], P('weight'), may hold values from -0.125 to 0.125
- up_blocks: bfloat16 [1792, 128, 128], P('weight'), may hold values from -0.125 to 0.125
- down_blocks: bfloat16 [1792, 128, 128], P('weight'), may hold values from -0.0625 to 0.0625
- row_starts: int32 [113], replicated, may hold values from 0 to 1792, as said below
- gate_cols: int32 [1792], P('weight'), may hold values from 0 to 31, as said below
- down_cols: int32 [1792], P('weight'), may hold values from 0 to 31, as said below
Outputs:
- mixed_out: bfloat16 [4, 64, 4096], P(None, ('groups', 'dp'), 'weight'), parts along dimension 1
There are 2 independent parts, one for each index of `groups`. A program takes and returns all parts, laid end to end along the dimension named above; an argument that names none is the same for every part. Nothing has to cross between parts.
Inputs may be any that keep to these rules, and one draw needn't show every extreme that they name: row_starts[0] = 0 and row_starts[112] = 1792; each row of blocks f holds row_starts[f+1] - row_starts[f] blocks, from 8 to 24, both reached; the down projection's rows of blocks hold the same counts as the gate's. `gate_cols`: within a row of blocks the entries rise strictly. `down_cols`: within a row of blocks (given by row_starts) the entries rise strictly.
All inputs are finite; a program needn't handle non-finite values.
Results may differ from a plain program's by a relative error of at most 0.017.
Values may be sent and summed in bfloat16 or wider, within the bound.
No kernel may reach another device: no remote copies, remote signals or barrier semaphores. Data moves between devices by JAX's collectives and lax.ppermute only.
A program may use at most 128 MiB of HBM per device.

v0:
```python
import jax
import jax.numpy as jnp
from jax import lax
from jax.sharding import PartitionSpec as P


def from_behind(value, axis, steps):
    count = lax.axis_size(axis)
    first, last = (max(0, -steps), min(count, count - steps))
    return lax.ppermute(value, axis, [(source, source + steps) for source in range(first, last)])


def place_terms(pattern, selector, values):
    upper_part = values.astype(jnp.bfloat16)
    lower_part = (values - upper_part.astype(jnp.float32)).astype(jnp.bfloat16)
    first_sum = jnp.einsum(pattern, selector, upper_part, preferred_element_type=jnp.float32)
    second_sum = jnp.einsum(pattern, selector, lower_part, preferred_element_type=jnp.float32)
    return first_sum + second_sum


def per_device(tokens, gate_blocks, up_blocks, down_blocks, row_starts, gate_cols, down_cols):
    per_dev, blk_width, _ = gate_blocks.shape
    model_width = tokens.shape[2]
    col_blocks = model_width // blk_width
    weight_size = lax.axis_size("weight")
    my_index = lax.axis_index("weight")
    first_block = my_index * per_dev
    global_index = first_block + jnp.arange(per_dev, dtype=jnp.int32)
    block_row = jnp.sum(
        (row_starts[1:][None, :] <= global_index[:, None]).astype(jnp.int32), axis=1
    )
    first_row = block_row[0]
    last_row = block_row[per_dev - 1]
    local_row = block_row - first_row
    last_local = last_row - first_row
    row_slots = (per_dev - 1) // (col_blocks // 4) + 2
    slot_ids = jnp.arange(row_slots, dtype=jnp.int32)
    row_place = (slot_ids[:, None] == local_row[None, :]).astype(jnp.bfloat16)
    enters = row_starts[first_row] < first_block
    leaves = row_starts[last_row + 1] > first_block + per_dev
    piece = lax.all_gather(tokens, "weight", axis=0, tiled=True)
    row_count = piece.shape[0] * piece.shape[1]
    by_column = piece.reshape(row_count, col_blocks, blk_width)
    picked = jnp.take(by_column, gate_cols, axis=1)
    gate_terms = jnp.einsum("rik,ikj->irj", picked, gate_blocks, preferred_element_type=jnp.float32)
    up_terms = jnp.einsum("rik,ikj->irj", picked, up_blocks, preferred_element_type=jnp.float32)
    gate_rows = place_terms("li,irj->lrj", row_place, gate_terms)
    up_rows = place_terms("li,irj->lrj", row_place, up_terms)
    row_sums = jnp.stack([gate_rows, up_rows])
    at_last = jnp.logical_and(leaves, slot_ids == last_local)[None, :, None, None]
    at_first = jnp.logical_and(enters, slot_ids == 0)
    incoming = from_behind(row_sums[:, 0].astype(jnp.bfloat16), "weight", -1).astype(jnp.float32)
    row_sums = jnp.where(at_last, row_sums + incoming[:, None], row_sums)
    hidden = (jax.nn.silu(row_sums[0]) * row_sums[1]).astype(jnp.bfloat16)
    tail_rows = lax.dynamic_index_in_dim(hidden, last_local, 0, keepdims=False)
    handed = from_behind(tail_rows, "weight", 1)
    hidden = jnp.where(at_first[:, None, None], handed[None], hidden)
    by_block = jnp.take(hidden, local_row, axis=0)
    token_total = by_block.shape[1]
    contrib = jnp.einsum("irk,ikj->irj", by_block, down_blocks, preferred_element_type=jnp.float32)
    target = (jnp.arange(col_blocks, dtype=jnp.int32)[:, None] == down_cols[None, :]).astype(
        jnp.bfloat16
    )
    partial_value = place_terms("di,irj->rdj", target, contrib).reshape(token_total, model_width)
    result = lax.psum_scatter(
        partial_value.astype(jnp.bfloat16), "weight", scatter_dimension=1, tiled=True
    ).astype(jnp.float32)
    return result.astype(jnp.bfloat16).reshape(
        weight_size, token_total // weight_size, result.shape[1]
    )


def solution(mesh):
    in_specs = (
        P("weight", ("groups", "dp"), None),
        P("weight", None, None),
        P("weight", None, None),
        P("weight", None, None),
        P(),
        P("weight"),
        P("weight"),
    )
    out_specs = P(None, ("groups", "dp"), "weight")
    return jax.shard_map(
        per_device, mesh=mesh, in_specs=in_specs, out_specs=out_specs, check_vma=False
    )
```

profile of v0, /device:TPU:0, one launch (start us, length us, event | category | flops | bytes accessed | tf_op | source)
XLA Modules:
  0.0 107.5 jit_solution(1962616222972767299)
XLA Ops:
  6.5 0.0 reduce-scatter.2.cloned.1.call-start
  6.5 0.7 compare_select_fusion.1
  7.2 0.7 compare_and_fusion
  7.9 0.7 slice.19
  8.6 0.2 convert_reduce_fusion
  8.9 0.6 fusion.59
  9.5 0.6 compare_and_fusion.3
  10.1 7.4 %all_gather.3 = bf16[4,8,4096]{2,1,0:T(8,128)(2,1)S(1)} all-gather(bf16[1,8,4096]{2,1,0:T(8,128)(2,1)} %param.7), channel_id=1, replica_groups=mesh['groups'=2,'weight'=4,'dp'=4] {'weight'}, dimensions={0}, use_global_device_ids=true | all-gather | bytes 327680 | tf_op jit(solution)/shard_map/all_gather | solution.py:41
  17.6 0.1 copy.40
  17.7 0.0 slice-start
  17.7 3.4 %gather_fusion = bf16[448,32,128]{2,1,0:T(8,128)(2,1)} fusion(bf16[32,32,128]{2,0,1:T(8,128)(2,1)S(1)} %copy.40, s32[1024]{0:T(1024)S(1)} %pad_clamp_fusion.1), kind=kCustom, calls=%fused_computation | custom fusion | bytes 7341824 | tf_op jit(solution)/shard_map/jit(_take)/gather | solution.py:44
  21.1 0.0 copy-start
  21.1 0.0 slice-start.1
  21.1 0.0 slice-start.2
  21.1 0.0 slice-start.3
  21.1 10.4 %subtract_convert_fusion.2 = (bf16[448,32,128]{2,1,0:T(8,128)(2,1)}, bf16[448,32,128]{2,1,0:T(8,128)(2,1)}) fusion(bf16[448,128,128]{2,1,0:T(8,128)(2,1)} %param.8, bf16[448,32,128]{2,1,0:T(8,128)(2,1)} %gather_fusion, pred[448]{0:T(512)(128)(4,1)S(1)} %compare_and_fusion), kind=kOutput, calls=%fused_computation.4 | convolution fusion | flops 478937088 | bytes 25690560 | tf_op jit(solution)/shard_map/rik,ikj->irj/dot_general | solution.py:45
  31.5 0.0 slice-done
  31.5 0.0 copy-done
  31.5 0.3 slice-done.1
  31.9 1.7 %slice-done.2 = s8[4194304]{0:T(1024)(128)(4,1)S(1)} async-done(((s8[14680064]{0:T(1024)(128)(4,1)}), s8[4194304]{0:T(1024)(128)(4,1)S(1)}, s32[]{:S(2)}) %slice-start.2) | async-done | bytes 4194328
  33.5 1.2 %slice-done.3 = s8[4194304]{0:T(1024)(128)(4,1)S(1)} async-done(((s8[14680064]{0:T(1024)(128)(4,1)}), s8[4194304]{0:T(1024)(128)(4,1)S(1)}, s32[]{:S(2)}) %slice-start.3) | async-done | bytes 4194328
  34.7 5.8 %subtract_convert_fusion.1 = (bf16[448,32,128]{2,1,0:T(8,128)(2,1)}, bf16[448,32,128]{2,1,0:T(8,128)(2,1)}) fusion(bf16[448,128,128]{2,1,0:T(8,128)(2,1)S(1)} %bitcast.62, bf16[448,32,128]{2,1,0:T(8,128)(2,1)S(1)} %copy-done, pred[448]{0:T(512)(128)(4,1)S(1)} %compare_and_fusion), kind=kOutput, calls=%fused_computation.3 | convolution fusion | flops 478937088 | bytes 25690560 | tf_op jit(solution)/shard_map/rik,ikj->irj/dot_general | solution.py:46
  40.5 0.0 copy-start.3
  40.5 0.0 copy-start.2
  40.5 3.5 %fusion.12 = f32[57,32,128]{2,0,1:T(8,128)S(1)} fusion(bf16[448,32,128]{2,1,0:T(8,128)(2,1)} %get-tuple-element.9, s32[448]{0:T(512)S(1)} %get-tuple-element.8), kind=kOutput, calls=%fused_computation.17 | convolution fusion | flops 209216448 | bytes 4605696 | tf_op jit(solution)/shard_map/li,irj->lrj/dot_general | solution.py:17
  44.0 0.0 copy-done.3
  44.0 1.3 %fusion.8 = f32[57,32,128]{2,0,1:T(8,128)S(1)} fusion(bf16[448,32,128]{2,1,0:T(8,128)(2,1)S(1)} %copy-done.3, s32[448]{0:T(512)S(1)} %get-tuple-element.8), kind=kOutput, calls=%fused_computation.13 | convolution fusion | flops 209216448 | bytes 4605696 | tf_op jit(solution)/shard_map/li,irj->lrj/dot_general | solution.py:17
  45.3 0.0 copy-start.1
  45.3 0.0 copy-done.2
  45.4 1.4 %fusion.23 = f32[1,57,32,128]{3,1,2,0:T(8,128)S(1)} fusion(f32[57,32,128]{2,0,1:T(8,128)S(1)} %fusion.12, bf16[448,32,128]{2,1,0:T(8,128)(2,1)S(1)} %copy-done.2, s32[448]{0:T(512)S(1)} %get-tuple-element.8), kind=kOutput, calls=%fused_computation.31 | convolution fusion | flops 209449920 | bytes 5539584 | tf_op jit(solution)/shard_map/li,irj->lrj/dot_general | solution.py:16
  46.7 0.7 copy-done.1
  47.4 0.0 copy-start.4
  47.4 1.3 %fusion.29 = f32[1,57,32,128]{3,1,2,0:T(8,128)S(1)} fusion(f32[57,32,128]{2,0,1:T(8,128)S(1)} %fusion.8, bf16[448,32,128]{2,1,0:T(8,128)(2,1)S(1)} %copy-done.1, s32[448]{0:T(512)S(1)} %get-tuple-element.8), kind=kOutput, calls=%fused_computation.33 | convolution fusion | flops 209449920 | bytes 5539584 | tf_op jit(solution)/shard_map/li,irj->lrj/dot_general | solution.py:16
  48.8 1.3 %collective-permute-start = (bf16[2,32,128]{2,1,0:T(8,128)(2,1)S(1)}, bf16[2,32,128]{2,1,0:T(8,128)(2,1)S(1)}, u32[]{:S(2)}, u32[]{:S(2)}) collective-permute-start(bf16[2,32,128]{2,1,0:T(8,128)(2,1)S(1)} %bitcast.68), channel_id=1, source_target_pairs={{4,0},{8,4},{12,8},{5,1},{9,5},{13,9},{6,2},{10,6},{14,10},{7,3},{... | collective-permute-start | bytes 49160 | tf_op jit(solution)/shard_map/ppermute | solution.py:10
  54.5 0.0 copy-done.4
  54.6 0.7 fusion.60
  56.6 0.0 collective-permute-done
  56.6 0.5 add_select_fusion
  57.1 0.3 fusion.39
  57.5 3.2 %collective-permute-start.1 = (bf16[32,128]{1,0:T(8,128)(2,1)S(1)}, bf16[32,128]{1,0:T(8,128)(2,1)S(1)}, u32[]{:S(2)}, u32[]{:S(2)}) collective-permute-start(bf16[32,128]{1,0:T(8,128)(2,1)S(1)} %bitcast.69), channel_id=1, source_target_pairs={{0,4},{4,8},{8,12},{1,5},{5,9},{9,13},{2,6},{6,10},{10,14},{3,7},{... | collective-permute-start | bytes 24584 | tf_op jit(solution)/shard_map/ppermute | solution.py:10
  60.7 0.6 collective-permute-done.1
  61.3 0.4 broadcast_select_fusion.3
  61.7 0.3 copy.45
  62.0 3.3 %gather_fusion.1 = bf16[448,32,128]{2,1,0:T(8,128)(2,1)} fusion(bf16[57,32,128]{2,1,0:T(8,128)(2,1)S(1)} %copy.45, s32[1024]{0:T(1024)S(1)} %pad_clamp_fusion), kind=kCustom, calls=%fused_computation.1 | custom fusion | bytes 7341824 | tf_op jit(solution)/shard_map/jit(_take)/gather | solution.py:58
  65.3 0.0 copy-start.5
  65.3 8.4 %subtract_convert_fusion = (bf16[448,32,128]{2,1,0:T(8,128)(2,1)S(1)}, bf16[448,32,128]{2,1,0:T(8,128)(2,1)S(1)}) fusion(bf16[448,128,128]{2,1,0:T(8,128)(2,1)} %param.10, bf16[448,32,128]{2,1,0:T(8,128)(2,1)} %gather_fusion.1, pred[448]{0:T(512)(128)(4,1)S(1)} %get-tuple-element.7), kind=kOutput, calls=%fused_computation.2 | convolution fusion | flops 478937088 | bytes 25690560 | tf_op jit(solution)/shard_map/irk,ikj->irj/dot_general | solution.py:60
  73.7 0.0 copy-done.5
  73.7 1.2 %fusion.4 = f32[32,128,32]{1,2,0:T(8,128)S(1)} fusion(bf16[448,32,128]{2,1,0:T(8,128)(2,1)S(1)} %get-tuple-element.5, s32[448]{0:T(512)S(1)} %copy-done.5), kind=kOutput, calls=%fused_computation.9 | convolution fusion | flops 117454848 | bytes 4196096 | tf_op jit(solution)/shard_map/di,irj->rdj/dot_general | solution.py:17
  74.9 1.2 %fusion.35 = bf16[32,128,32]{1,2,0:T(8,128)(2,1)S(1)} fusion(f32[32,128,32]{1,2,0:T(8,128)S(1)} %fusion.4, bf16[448,32,128]{2,1,0:T(8,128)(2,1)S(1)} %get-tuple-element.6, s32[448]{0:T(512)S(1)} %copy-done.5), kind=kOutput, calls=%fused_computation.35 | convolution fusion | flops 117716992 | bytes 4458240 | tf_op jit(solution)/shard_map/di,irj->rdj/dot_general | solution.py:16
  76.1 0.8 copy.79
  76.9 0.0 reduce-scatter.2.cloned.1.call-update
  76.9 23.7 %reduce-scatter.2.cloned.1.call-done = bf16[32,1024]{1,0:T(8,128)(2,1)} async-done(((bf16[32,4096]{1,0:T(8,128)(2,1)}), bf16[32,1024]{1,0:T(8,128)(2,1)}) %reduce-scatter.2.cloned.1.call-update) | async-done | bytes 65552 | tf_op jit(solution)/shard_map/reduce_scatter | solution.py:65
  (13 shorter events, 0.2 us)
Async XLA Ops:
  6.5 94.1 %reduce-scatter.2.cloned.1.call-start = ((), (), s32[]{:S(2)}) async-start(), calls=%async_computation.1 | async-start | bytes 327680 | tf_op jit(solution)/shard_map/reduce_scatter | solution.py:65
  17.7 13.8 %slice-start = ((s8[14680064]{0:T(1024)(128)(4,1)}), s8[2097152]{0:T(1024)(128)(4,1)S(1)}, s32[]{:S(2)}) async-start(s8[14680064]{0:T(1024)(128)(4,1)} %bitcast.61), calls=%async_computation.2 | async-start | bytes 4194304
  21.1 10.4 %copy-start = (bf16[448,32,128]{2,1,0:T(8,128)(2,1)S(1)}, bf16[448,32,128]{2,1,0:T(8,128)(2,1)}, u32[]{:S(2)}) copy-start(bf16[448,32,128]{2,1,0:T(8,128)(2,1)} %gather_fusion) | copy-start | bytes 11010052
  21.1 10.7 %slice-start.1 = ((s8[14680064]{0:T(1024)(128)(4,1)}), s8[4194304]{0:T(1024)(128)(4,1)S(1)}, s32[]{:S(2)}) async-start(s8[14680064]{0:T(1024)(128)(4,1)} %bitcast.61), calls=%async_computation.3 | async-start | bytes 8388608
  21.1 12.4 %slice-start.2 = ((s8[14680064]{0:T(1024)(128)(4,1)}), s8[4194304]{0:T(1024)(128)(4,1)S(1)}, s32[]{:S(2)}) async-start(s8[14680064]{0:T(1024)(128)(4,1)} %bitcast.61), calls=%async_computation.4 | async-start | bytes 8388608
  21.1 13.6 %slice-start.3 = ((s8[14680064]{0:T(1024)(128)(4,1)}), s8[4194304]{0:T(1024)(128)(4,1)S(1)}, s32[]{:S(2)}) async-start(s8[14680064]{0:T(1024)(128)(4,1)} %bitcast.61), calls=%async_computation.5 | async-start | bytes 8388608
  40.5 3.5 %copy-start.3 = (bf16[448,32,128]{2,1,0:T(8,128)(2,1)S(1)}, bf16[448,32,128]{2,1,0:T(8,128)(2,1)}, u32[]{:S(2)}) copy-start(bf16[448,32,128]{2,1,0:T(8,128)(2,1)} %get-tuple-element.11) | copy-start | bytes 11010052
  40.5 4.8 %copy-start.2 = (bf16[448,32,128]{2,1,0:T(8,128)(2,1)S(1)}, bf16[448,32,128]{2,1,0:T(8,128)(2,1)}, u32[]{:S(2)}) copy-start(bf16[448,32,128]{2,1,0:T(8,128)(2,1)} %get-tuple-element.10) | copy-start | bytes 11010052
  45.3 2.0 %copy-start.1 = (bf16[448,32,128]{2,1,0:T(8,128)(2,1)S(1)}, bf16[448,32,128]{2,1,0:T(8,128)(2,1)}, u32[]{:S(2)}) copy-start(bf16[448,32,128]{2,1,0:T(8,128)(2,1)} %get-tuple-element.12) | copy-start | bytes 11010052
  47.4 7.2 %copy-start.4 = (s32[113]{0:T(128)S(1)}, s32[113]{0:T(128)}, u32[]{:S(2)}) copy-start(s32[113]{0:T(128)} %param.11) | copy-start | bytes 1360
  48.8 7.8 %collective-permute-start = (bf16[2,32,128]{2,1,0:T(8,128)(2,1)S(1)}, bf16[2,32,128]{2,1,0:T(8,128)(2,1)S(1)}, u32[]{:S(2)}, u32[]{:S(2)}) collective-permute-start(bf16[2,32,128]{2,1,0:T(8,128)(2,1)S(1)} %bitcast.68), channel_id=1, source_target_pairs={{4,0},{8,4},{12,8},{5,1},{9,5},{13,9},{6,2},{10,6},{14,10},{7,3},{... | collective-permute-start | bytes 49160 | tf_op jit(solution)/shard_map/ppermute | solution.py:10
  57.5 3.8 %collective-permute-start.1 = (bf16[32,128]{1,0:T(8,128)(2,1)S(1)}, bf16[32,128]{1,0:T(8,128)(2,1)S(1)}, u32[]{:S(2)}, u32[]{:S(2)}) collective-permute-start(bf16[32,128]{1,0:T(8,128)(2,1)S(1)} %bitcast.69), channel_id=1, source_target_pairs={{0,4},{4,8},{8,12},{1,5},{5,9},{9,13},{2,6},{6,10},{10,14},{3,7},{... | collective-permute-start | bytes 24584 | tf_op jit(solution)/shard_map/ppermute | solution.py:10
  65.3 8.4 %copy-start.5 = (s32[448]{0:T(512)S(1)}, s32[448]{0:T(512)}, u32[]{:S(2)}) copy-start(s32[448]{0:T(512)} %param.13) | copy-start | bytes 5380
Sparse Core Ops, SparseCore 0:
  77.0 23.5 reduce-scatter.1
where the time goes:
time: 108 us; the launch traced here: 107 us
  matrix products  34.5 us (32%)
  waiting for transfers between devices  24.3 us (22%)
  between operations  19.4 us (18%)
  local copies, waits for them, and re-layouts  13.9 us (13%)
  blocking collectives  7.41 us (7%)
  starting transfers between devices  4.51 us (4%)
  other arithmetic  3.47 us (3%)
    reduce_scatter x1, waiting for transfers between devices, per_device(): lax.psum_scatter(partial_value.astype(jnp.bfloat16), 'weight', scatter_di...  23.7 us
    dot_general x1, matrix products, per_device(): jnp.einsum('rik,ikj->irj', picked, gate_blocks, preferred_element_type=jn...  10.4 us
    dot_general x1, matrix products, per_device(): jnp.einsum('irk,ikj->irj', by_block, down_blocks, preferred_element_type=...  8.37 us
    all_gather x1, blocking collectives, per_device(): piece = lax.all_gather(tokens, 'weight', axis=0, tiled=True)  7.41 us
    dot_general x3, matrix products, place_terms(): jnp.einsum(pattern, selector, lower_part, preferred_element_type=jnp.floa...  5.98 us
    dot_general x1, matrix products, per_device(): jnp.einsum('rik,ikj->irj', picked, up_blocks, preferred_element_type=jnp....  5.83 us
    unnamed x24, local copies, waits for them, and re-layouts  4.73 us
    ppermute x2, starting transfers between devices, from_behind(): lax.ppermute(value, axis, [(source, source + steps) for source in range(f...  4.5 us
  transfers between devices with their start and end apart: 3, of which 2 were waited for; matrix products, arithmetic and copies ran while one was open for 1% of the time, Pallas kernels for 0%

commit v1 on v0

v1 whole, which is shorter than its diff:
```python
import functools

import jax
import jax.numpy as jnp
from jax import lax
from jax.experimental import pallas as pl
from jax.experimental.pallas import tpu as pltpu
from jax.sharding import PartitionSpec as P

GROUP = 8
EDGE = 24
VM = pl.BlockSpec(memory_space=pltpu.VMEM)
SM = pl.BlockSpec(memory_space=pltpu.SMEM)
HB = pl.BlockSpec(memory_space=pltpu.HBM)
F32 = jnp.float32
BF16 = jnp.bfloat16


def limit(mib):
    return pltpu.CompilerParams(vmem_limit_bytes=mib * 2**20)


def cost(flops):
    return pl.CostEstimate(flops=flops, bytes_accessed=2**20, transcendentals=0)


def largest_unroll(steps, most):
    return max(u for u in range(1, most + 1) if steps % u == 0)


def in_vmem(value):
    return pltpu.with_memory_space_constraint(value, pltpu.VMEM)


def in_hbm(value):
    return pltpu.with_memory_space_constraint(value, pltpu.HBM)


def prepare_kernel(starts, gate, up, slots, edge_gate, edge_up, sems, *, count):
    copies = []
    for k, (source, target) in enumerate(((gate, edge_gate), (up, edge_up))):
        for side, first in enumerate((0, count - EDGE)):
            copies.append(
                pltpu.make_async_copy(source.at[pl.ds(first, EDGE)], target.at[side], sems.at[k, side])
            )
    for copy in copies:
        copy.start()
    first_block = lax.axis_index("weight") * count
    lanes = lax.broadcasted_iota(jnp.int32, slots.shape, 1)
    place = first_block + lax.broadcasted_iota(jnp.int32, slots.shape, 0) * 128 + lanes
    row = jnp.zeros(slots.shape, jnp.int32)
    first_row, enters, leaves = 0, 1, 1
    for f in range(1, starts.shape[0]):
        start = starts[f]
        row += (start <= place).astype(jnp.int32)
        first_row += (start <= first_block).astype(jnp.int32)
        enters = jnp.where(start == first_block, 0, enters)
        leaves = jnp.where(start == first_block + count, 0, leaves)
    enters = jnp.where(first_block == 0, 0, enters)
    flag_row = lax.broadcasted_iota(jnp.int32, slots.shape, 0) == slots.shape[0] - 1
    slots[...] = jnp.where(flag_row, jnp.where(lanes == 0, enters, leaves), row - first_row)
    for copy in copies:
        copy.wait()


def slot_of(slots, block):
    if isinstance(block, int):
        return slots[block // 128, block % 128]
    return slots[lax.shift_right_logical(block, 7), lax.bitwise_and(block, 127)]


def edge_kernel(slots, cols, *refs):
    pieces, (edge_gate, edge_up, by_col, to_prev, to_next, whole) = refs[:-6], refs[-6:]
    size = len(pieces)
    count = cols.shape[0]
    col_blocks, rows = by_col.shape[0] - 1, by_col.shape[1]
    me = lax.axis_index("weight")
    for step, piece in enumerate(pieces):
        whole[lax.rem(me + size - step, size)] = piece[0]
    merged = whole[...].reshape(rows, col_blocks * 128)
    for c in range(col_blocks):
        by_col[c] = merged[:, c * 128 : (c + 1) * 128]
    by_col[col_blocks] = jnp.zeros((rows, 128), BF16)
    last_flag = slots.shape[0] - 1
    for side, first, sent in ((0, 0, to_prev), (1, count - EDGE, to_next)):
        mine = slot_of(slots, 0 if side == 0 else count - 1)
        picked = []
        for q in range(EDGE):
            block = first + q
            picked.append(by_col[jnp.where(slot_of(slots, block) == mine, cols[block], col_blocks)])
        weights = jnp.concatenate(
            [edge_gate[side].reshape(EDGE * 128, 128), edge_up[side].reshape(EDGE * 128, 128)], axis=1
        )
        total = jnp.dot(jnp.concatenate(picked, axis=1), weights, preferred_element_type=F32)
        sent[...] = jnp.where(slots[last_flag, side] == 1, total, 0.0).astype(BF16)


def silu_gate(sums):
    gate, up = sums[..., :128], sums[..., 128:]
    return (gate / (1 + jnp.exp(-gate)) * up).astype(BF16)


def hidden_kernel(slots, cols, by_col, gate, up, hidden, edges, sums, *, unroll):
    col_blocks, rows = by_col.shape[0] - 1, by_col.shape[1]
    count = cols.shape[0]
    sums[...] = jnp.zeros_like(sums)

    def step(it, carry):
        for j in range(unroll):
            first = (it * unroll + j) * GROUP
            slot = slot_of(slots, first)
            even, odd = [], []
            for q in range(GROUP):
                col, is_odd = cols[first + q], (slot_of(slots, first + q) & 1) == 1
                even.append(by_col[jnp.where(is_odd, col_blocks, col)])
                odd.append(by_col[jnp.where(is_odd, col, col_blocks)])
            left = jnp.concatenate([jnp.concatenate(even, axis=1), jnp.concatenate(odd, axis=1)], axis=0)
            right = jnp.concatenate(
                [ref[pl.ds(first, GROUP)].reshape(GROUP * 128, 128) for ref in (gate, up)], axis=1
            )
            part = jnp.dot(left, right, preferred_element_type=F32)
            at_even, at_odd = slot + (slot & 1), slot | 1
            old_even, old_odd = sums[at_even], sums[at_odd]
            sums[at_even] = old_even + part[:rows]
            sums[at_odd] = old_odd + part[rows:]
        return carry

    lax.fori_loop(0, count // GROUP // unroll, step, 0)
    hidden[...] = silu_gate(sums[...])
    edges[0] = sums[0]
    edges[1] = sums[slot_of(slots, count - 1)]


def down_kernel(slots, cols, hidden, edges, from_prev, from_next, down, *refs, unroll):
    outs, (rows_in, sums) = refs[:-2], refs[-2:]
    size = len(outs)
    count = cols.shape[0]
    rows = hidden.shape[1]
    col_blocks = sums.shape[1]
    rows_in[...] = hidden[...]
    rows_in[0] = silu_gate(edges[0] + from_prev[...].astype(F32))
    rows_in[slot_of(slots, count - 1)] = silu_gate(edges[1] + from_next[...].astype(F32))
    sums[...] = jnp.zeros_like(sums)

    def step(it, carry):
        for j in range(unroll):
            first = (it * unroll + j) * GROUP
            slot = slot_of(slots, first)
            left = jnp.concatenate([rows_in[slot + (slot & 1)], rows_in[slot | 1]], axis=0)
            right = jnp.concatenate([down[first + q] for q in range(GROUP)], axis=1)
            part = jnp.dot(left, right, preferred_element_type=F32)
            for half in range(0, GROUP, 4):
                at = [(slot_of(slots, first + q) & 1, cols[first + q]) for q in range(half, half + 4)]
                old = [sums[odd, col] for odd, col in at]
                for q, (odd, col) in enumerate(at):
                    term = part[:, (half + q) * 128 : (half + q + 1) * 128]
                    sums[odd, col] = old[q] + jnp.where(odd == 1, term[rows:], term[:rows])
        return carry

    lax.fori_loop(0, count // GROUP // unroll, step, 0)
    me = lax.axis_index("weight")
    share = col_blocks // size
    for distance, out in enumerate(outs):
        first = lax.rem(me + distance, size) * share
        for c in range(share):
            total = sums[0, first + c] + sums[1, first + c]
            out[:, c * 128 : (c + 1) * 128] = total.astype(out.dtype)


def per_device(tokens, gate_blocks, up_blocks, down_blocks, row_starts, gate_cols, down_cols):
    count, width, _ = gate_blocks.shape
    model_width = tokens.shape[2]
    col_blocks = model_width // width
    size = lax.axis_size("weight")
    slab = tokens.shape[1]
    rows = size * slab
    row_slots = (count - 1) // GROUP + 3

    def shift(value, distance):
        return lax.ppermute(value, "weight", [(d, (d + distance) % size) for d in range(size)])

    pieces = [tokens] + [shift(tokens, distance) for distance in range(1, size)]
    slot_rows = -(-count // 128) + 1
    slots, edge_gate, edge_up = pl.pallas_call(
        functools.partial(prepare_kernel, count=count),
        out_shape=(
            jax.ShapeDtypeStruct((slot_rows, 128), jnp.int32),
            pltpu.VMEM((2, EDGE, width, width), BF16),
            pltpu.VMEM((2, EDGE, width, width), BF16),
        ),
        in_specs=[SM, HB, HB],
        out_specs=(VM, VM, VM),
        scratch_shapes=[pltpu.SemaphoreType.DMA((2, 2))],
        compiler_params=limit(4),
        cost_estimate=cost(2**36),
        name="prepare",
    )(row_starts, in_hbm(gate_blocks), in_hbm(up_blocks))
    by_col, to_prev, to_next = pl.pallas_call(
        edge_kernel,
        out_shape=(
            pltpu.VMEM((col_blocks + 1, rows, width), BF16),
            jax.ShapeDtypeStruct((rows, 2 * width), BF16),
            jax.ShapeDtypeStruct((rows, 2 * width), BF16),
        ),
        in_specs=[SM, SM] + [VM] * (size + 2),
        out_specs=(VM, VM, VM),
        scratch_shapes=[pltpu.VMEM((size, slab, model_width), BF16)],
        compiler_params=limit(4),
        name="edges",
    )(slots, gate_cols, *pieces, edge_gate, edge_up)
    from_next = lax.ppermute(to_prev, "weight", [(d + 1, d) for d in range(size - 1)])
    from_prev = lax.ppermute(to_next, "weight", [(d, d + 1) for d in range(size - 1)])
    hidden, edges = pl.pallas_call(
        functools.partial(hidden_kernel, unroll=largest_unroll(count // GROUP, 28)),
        out_shape=(
            pltpu.VMEM((row_slots, rows, width), BF16),
            pltpu.VMEM((2, rows, 2 * width), F32),
        ),
        in_specs=[SM, SM, VM, VM, VM],
        out_specs=(VM, VM),
        scratch_shapes=[pltpu.VMEM((row_slots, rows, 2 * width), F32)],
        compiler_params=limit(8),
        cost_estimate=cost(2**30),
        name="hidden",
    )(slots, gate_cols, by_col, in_vmem(gate_blocks), in_vmem(up_blocks))
    outs = pl.pallas_call(
        functools.partial(down_kernel, unroll=largest_unroll(count // GROUP, 28)),
        out_shape=tuple(
            jax.ShapeDtypeStruct((rows, model_width // size), BF16 if distance else F32)
            for distance in range(size)
        ),
        in_specs=[SM, SM] + [VM] * 5,
        out_specs=(VM,) * size,
        scratch_shapes=[
            pltpu.VMEM((row_slots, rows, width), BF16),
            pltpu.VMEM((2, col_blocks, rows, width), F32),
        ],
        compiler_params=limit(8),
        name="down",
    )(slots, down_cols, hidden, edges, from_prev, from_next, in_vmem(down_blocks))
    total = outs[0]
    for distance in range(1, size):
        total = total + shift(outs[distance], distance).astype(F32)
    return total.astype(BF16).reshape(size, slab, model_width // size)


def solution(mesh):
    in_specs = (
        P("weight", ("groups", "dp"), None),
        P("weight", None, None),
        P("weight", None, None),
        P("weight", None, None),
        P(),
        P("weight"),
        P("weight"),
    )
    out_specs = P(None, ("groups", "dp"), "weight")
    return jax.shard_map(
        per_device, mesh=mesh, in_specs=in_specs, out_specs=out_specs, check_vma=False
    )
```

time: 108 us -> 30.7 us (0.28)
  matrix products: 34.5 us -> 0 us
  waiting for transfers between devices: 24.3 us -> 1.92 us
  between operations: 19.4 us -> 0.21 us
  Pallas kernels: 0 us -> 13.7 us
  local copies, waits for them, and re-layouts: 13.9 us -> 1.45 us
  starting transfers between devices: 4.51 us -> 12.5 us
  blocking collectives: 7.41 us -> 0 us
  other arithmetic: 3.47 us -> 0.66 us
    dot_general x9 -> x0, matrix products: 34.5 us -> none  [the longest x1 10.4 us: per_device(): jnp.einsum('rik,ikj->irj', picked, gate_blocks, preferred_element_type=jn...]
    reduce_scatter x1 -> x0, waiting for transfers between devices: 23.7 us -> none  [per_device(): lax.psum_scatter(partial_value.astype(jnp.bfloat16), 'weight', scatter_di...]
    pallas_call x0 -> x4, Pallas kernels: none -> 13.7 us  [the longest x1 6.35 us: per_device(): pl.pallas_call(functools.partial(hidden_kernel, unroll=largest_unroll(cou...]
    ppermute x2 -> x8, starting transfers between devices: 4.5 us -> 12.5 us  [the longest x6 9.81 us: shift(): lax.ppermute(value, 'weight', [(d, (d + distance) % size) for d in range(...]
    all_gather x1 -> x0, blocking collectives: 7.41 us -> none  [per_device(): piece = lax.all_gather(tokens, 'weight', axis=0, tiled=True)]
    gather x2 -> x0, local copies, waits for them, and re-layouts: 6.71 us -> none  [the longest x1 3.42 us: per_device(): picked = jnp.take(by_column, gate_cols, axis=1)]
    unnamed x24 -> x20, local copies, waits for them, and re-layouts: 4.73 us -> 1.45 us
    select_n x4 -> x0, other arithmetic: 1.56 us -> none  [the longest x1 0.68 us: per_device(): picked = jnp.take(by_column, gate_cols, axis=1)]
  transfers between devices with their start and end apart: 3 -> 8, of which waited for: 2 -> 2; matrix products, arithmetic and copies ran while one was open for 1% -> 0% of each run, Pallas kernels for 0% -> 30%
where the time goes in v1:
time: 30.7 us; the launch traced here: 30.5 us
  Pallas kernels  13.7 us (45%)
  starting transfers between devices  12.5 us (41%)
  waiting for transfers between devices  1.92 us (6%)
  local copies, waits for them, and re-layouts  1.45 us (5%)
  other arithmetic  0.66 us (2%)
    ppermute x6, starting transfers between devices, shift(): lax.ppermute(value, 'weight', [(d, (d + distance) % size) for d in range(...  9.81 us
    pallas_call x1, Pallas kernels, per_device(): pl.pallas_call(functools.partial(hidden_kernel, unroll=largest_unroll(cou...  6.35 us
    pallas_call x1, Pallas kernels, per_device(): pl.pallas_call(functools.partial(down_kernel, unroll=largest_unroll(count...  3.11 us
    pallas_call x1, Pallas kernels, per_device(): pl.pallas_call(functools.partial(prepare_kernel, count=count), out_shape=...  2.89 us
    ppermute x6, waiting for transfers between devices, shift(): lax.ppermute(value, 'weight', [(d, (d + distance) % size) for d in range(...  1.91 us
    unnamed x20, local copies, waits for them, and re-layouts  1.45 us
    ppermute x1, starting transfers between devices, per_device(): lax.ppermute(to_next, 'weight', [(d, d + 1) for d in range(size - 1)])  1.42 us
    pallas_call x1, Pallas kernels, per_device(): pl.pallas_call(edge_kernel, out_shape=(pltpu.VMEM((col_blocks + 1, rows,...  1.33 us
  transfers between devices with their start and end apart: 8, of which 2 were waited for; matrix products, arithmetic and copies ran while one was open for 0% of the time, Pallas kernels for 30%

profile of v1, /device:TPU:0, one launch (start us, length us, event | category | flops | bytes accessed | tf_op | source)
XLA Modules:
  0.0 30.5 jit_solution(11526736354112903873)
XLA Ops:
  0.0 0.0 copy-start.2
  0.0 0.0 copy-start.1
  0.0 0.0 copy-start
  0.0 0.0 copy-start.3
  0.0 3.0 %collective-permute-start.1 = (bf16[1,8,4096]{2,1,0:T(8,128)(2,1)}, bf16[1,8,4096]{2,1,0:T(8,128)(2,1)S(1)}, u32[]{:S(2)}, u32[]{:S(2)}) collective-permute-start(bf16[1,8,4096]{2,1,0:T(8,128)(2,1)} %refs_0_.1), channel_id=1, source_target_pairs={{0,8},{4,12},{8,0},{12,4},{1,9},{5,13},{9,1},{13,5},{2,10},{6,14},... | collective-permute-start | bytes 196616 | tf_op jit(solution)/shard_map/ppermute | solution.py:180
  3.0 0.0 collective-permute-start
  3.0 1.7 %collective-permute-start.2 = (bf16[1,8,4096]{2,1,0:T(8,128)(2,1)}, bf16[1,8,4096]{2,1,0:T(8,128)(2,1)S(1)}, u32[]{:S(2)}, u32[]{:S(2)}) collective-permute-start(bf16[1,8,4096]{2,1,0:T(8,128)(2,1)} %refs_0_.1), channel_id=1, source_target_pairs={{0,12},{4,0},{8,4},{12,8},{1,13},{5,1},{9,5},{13,9},{2,14},{6,2},{... | collective-permute-start | bytes 196616 | tf_op jit(solution)/shard_map/ppermute | solution.py:180
  4.8 0.0 copy-start.5
  4.8 1.4 %copy-done.5 = s32[113]{0:T(128)S(1)} copy-done((s32[113]{0:T(128)S(1)}, s32[113]{0:T(128)}, u32[]{:S(2)}) %copy-start.5) | copy-done | bytes 476
  6.2 2.9 %prepare.1 = (s32[5,128]{1,0:T(8,128)S(1)}, bf16[2,24,128,128]{3,2,1,0:T(8,128)(2,1)S(1)}, bf16[2,24,128,128]{3,2,1,0:T(8,128)(2,1)S(1)}) custom-call(s32[113]{0:T(128)S(1)} %copy-done.5, bf16[448,128,128]{2,1,0:T(8,128)(2,1)} %gate.3, bf16[448,128,128]{2,1,0:T(8,128)(2,1)} %up.3), custom_call_target="tpu_custom_call" | custom-call | flops 68719476736 | bytes 1048576 | tf_op jit(solution)/shard_map/prepare/pallas_call | solution.py:184
  9.1 0.0 collective-permute-done.1.refs_2_
  9.1 0.0 collective-permute-done.refs_1_
  9.1 0.0 collective-permute-done.2.refs_3_
  9.1 0.0 copy-done.2
  9.1 0.0 copy-done.3
  9.1 0.0 slice-start
  9.1 1.3 %edges.1 = (bf16[33,32,128]{2,1,0:T(8,128)(2,1)S(1)}, bf16[32,256]{1,0:T(8,128)(2,1)S(1)}, bf16[32,256]{1,0:T(8,128)(2,1)S(1)}) custom-call(s32[5,128]{1,0:T(8,128)S(1)} %get-tuple-element.17.slots, s32[448]{0:T(512)S(1)} %copy-done.3, bf16[1,8,4096]{2,1,0:T(8,128)(2,1)S(1)} %copy-done.2, bf16[1,8,4096]{2,1,0:T(8,128)(2,1)S(1)} %collective-permute-done.refs_1_, ...), custom_call_target="tpu_custom_call" | custom-call | tf_op jit(solution)/shard_map/edges/pallas_call | solution.py:198
  10.5 1.4 %collective-permute-start.3 = (bf16[32,256]{1,0:T(8,128)(2,1)S(1)}, bf16[32,256]{1,0:T(8,128)(2,1)S(1)}, u32[]{:S(2)}, u32[]{:S(2)}) collective-permute-start(bf16[32,256]{1,0:T(8,128)(2,1)S(1)} %get-tuple-element.23), channel_id=1, source_target_pairs={{0,4},{4,8},{8,12},{1,5},{5,9},{9,13},{2,6},{6,10},{10,14},{3,7},{... | collective-permute-start | bytes 49160 | tf_op jit(solution)/shard_map/ppermute | solution.py:212
  11.9 1.3 %collective-permute-start.4 = (bf16[32,256]{1,0:T(8,128)(2,1)S(1)}, bf16[32,256]{1,0:T(8,128)(2,1)S(1)}, u32[]{:S(2)}, u32[]{:S(2)}) collective-permute-start(bf16[32,256]{1,0:T(8,128)(2,1)S(1)} %get-tuple-element.24), channel_id=1, source_target_pairs={{4,0},{8,4},{12,8},{5,1},{9,5},{13,9},{6,2},{10,6},{14,10},{7,3},{... | collective-permute-start | bytes 49160 | tf_op jit(solution)/shard_map/ppermute | solution.py:211
  13.2 0.0 copy-done.1
  13.2 0.0 copy-done
  13.2 0.0 slice-start.1
  13.2 0.0 slice-start.2
  13.3 0.0 slice-start.3
  13.3 0.0 copy-start.4
  13.3 6.4 %hidden.1 = (bf16[58,32,128]{2,1,0:T(8,128)(2,1)S(1)}, f32[2,32,256]{2,1,0:T(8,128)S(1)}) custom-call(s32[5,128]{1,0:T(8,128)S(1)} %get-tuple-element.17.slots, s32[448]{0:T(512)S(1)} %copy-done.3, bf16[33,32,128]{2,1,0:T(8,128)(2,1)S(1)} %get-tuple-element.20.by_col, bf16[448,128,128]{2,1,0:T(8,128)(2,1)S(1)} %copy-done, bf16[448,128,128]{2,1,0:T(8,128)(2,1)S(1)} %copy-done.1), custom_call_target="tpu_custom_call" | custom-call | flops 1073741824 | bytes 1048576 | tf_op jit(solution)/shard_map/hidden/pallas_call | solution.py:213
  19.6 0.0 collective-permute-done.3.from_prev
  19.7 0.0 collective-permute-done.4.from_next
  19.7 0.0 slice-done
  19.7 0.0 slice-done.1
  19.7 0.0 slice-done.2
  19.7 0.0 slice-done.3
  19.7 0.0 copy-done.4
  19.7 3.1 %down.2 = (f32[32,1024]{1,0:T(8,128)S(1)}, bf16[32,1024]{1,0:T(8,128)(2,1)S(1)}, bf16[32,1024]{1,0:T(8,128)(2,1)S(1)}, bf16[32,1024]{1,0:T(8,128)(2,1)S(1)}) custom-call(s32[5,128]{1,0:T(8,128)S(1)} %get-tuple-element.17.slots, s32[448]{0:T(512)S(1)} %copy-done.4, bf16[58,32,128]{2,1,0:T(8,128)(2,1)S(1)} %get-tuple-element.21.hidden, ...), custom_call_target="tpu_custom_call" | custom-call | tf_op jit(solution)/shard_map/down/pallas_call | solution.py:226
  22.8 1.9 %collective-permute-start.5 = (bf16[32,1024]{1,0:T(8,128)(2,1)S(1)}, bf16[32,1024]{1,0:T(8,128)(2,1)S(1)}, u32[]{:S(2)}, u32[]{:S(2)}) collective-permute-start(bf16[32,1024]{1,0:T(8,128)(2,1)S(1)} %get-tuple-element.26), channel_id=1, source_target_pairs={{0,4},{4,8},{8,12},{12,0},{1,5},{5,9},{9,13},{13,1},{2,6},{6,10},{... | collective-permute-start | bytes 196616 | tf_op jit(solution)/shard_map/ppermute | solution.py:180
  24.8 1.7 %collective-permute-start.6 = (bf16[32,1024]{1,0:T(8,128)(2,1)S(1)}, bf16[32,1024]{1,0:T(8,128)(2,1)S(1)}, u32[]{:S(2)}, u32[]{:S(2)}) collective-permute-start(bf16[32,1024]{1,0:T(8,128)(2,1)S(1)} %get-tuple-element.27), channel_id=1, source_target_pairs={{0,8},{4,12},{8,0},{12,4},{1,9},{5,13},{9,1},{13,5},{2,10},{6,14},... | collective-permute-start | bytes 196616 | tf_op jit(solution)/shard_map/ppermute | solution.py:180
  26.5 1.4 %collective-permute-start.7 = (bf16[32,1024]{1,0:T(8,128)(2,1)S(1)}, bf16[32,1024]{1,0:T(8,128)(2,1)S(1)}, u32[]{:S(2)}, u32[]{:S(2)}) collective-permute-start(bf16[32,1024]{1,0:T(8,128)(2,1)S(1)} %get-tuple-element.28), channel_id=1, source_target_pairs={{0,12},{4,0},{8,4},{12,8},{1,13},{5,1},{9,5},{13,9},{2,14},{6,2},{... | collective-permute-start | bytes 196616 | tf_op jit(solution)/shard_map/ppermute | solution.py:180
  27.9 0.0 collective-permute-done.5
  27.9 1.2 %collective-permute-done.6 = bf16[32,1024]{1,0:T(8,128)(2,1)S(1)} collective-permute-done((bf16[32,1024]{1,0:T(8,128)(2,1)S(1)}, bf16[32,1024]{1,0:T(8,128)(2,1)S(1)}, u32[]{:S(2)}, u32[]{:S(2)}) %collective-permute-start.6) | collective-permute-done | bytes 65568 | tf_op jit(solution)/shard_map/ppermute | solution.py:180
  29.0 0.8 %collective-permute-done.7 = bf16[32,1024]{1,0:T(8,128)(2,1)S(1)} collective-permute-done((bf16[32,1024]{1,0:T(8,128)(2,1)S(1)}, bf16[32,1024]{1,0:T(8,128)(2,1)S(1)}, u32[]{:S(2)}, u32[]{:S(2)}) %collective-permute-start.7) | collective-permute-done | bytes 65568 | tf_op jit(solution)/shard_map/ppermute | solution.py:180
  29.8 0.7 %fusion = bf16[4,8,1024]{2,1,0:T(8,128)(2,1)} fusion(bf16[32,1024]{1,0:T(8,128)(2,1)S(1)} %collective-permute-done.7, bf16[32,1024]{1,0:T(8,128)(2,1)S(1)} %collective-permute-done.6, f32[32,1024]{1,0:T(8,128)S(1)} %get-tuple-element.25, bf16[32,1024]{1,0:T(8,128)(2,1)S(1)} %collective-permute-done.5), kind=kLoop, calls=%fused_computation.1 | loop fusion | flops 229376 | bytes 393216 | tf_op jit(solution)/shard_map/reshape | solution.py:244
  (1 shorter events, 0.0 us)
Async XLA Ops:
  0.0 9.1 %copy-start.2 = (bf16[1,8,4096]{2,1,0:T(8,128)(2,1)S(1)}, bf16[1,8,4096]{2,1,0:T(8,128)(2,1)}, u32[]{:S(2)}) copy-start(bf16[1,8,4096]{2,1,0:T(8,128)(2,1)} %refs_0_.1) | copy-start | bytes 196612
  0.0 13.2 %copy-start.1 = (bf16[448,128,128]{2,1,0:T(8,128)(2,1)S(1)}, bf16[448,128,128]{2,1,0:T(8,128)(2,1)}, u32[]{:S(2)}) copy-start(bf16[448,128,128]{2,1,0:T(8,128)(2,1)} %up.3) | copy-start | bytes 44040196
  0.0 13.2 %copy-start = (bf16[448,128,128]{2,1,0:T(8,128)(2,1)S(1)}, bf16[448,128,128]{2,1,0:T(8,128)(2,1)}, u32[]{:S(2)}) copy-start(bf16[448,128,128]{2,1,0:T(8,128)(2,1)} %gate.3) | copy-start | bytes 44040196
  0.0 9.1 %copy-start.3 = (s32[448]{0:T(512)S(1)}, s32[448]{0:T(512)}, u32[]{:S(2)}) copy-start(s32[448]{0:T(512)} %cols.4) | copy-start | bytes 5380
  0.0 9.1 %collective-permute-start.1 = (bf16[1,8,4096]{2,1,0:T(8,128)(2,1)}, bf16[1,8,4096]{2,1,0:T(8,128)(2,1)S(1)}, u32[]{:S(2)}, u32[]{:S(2)}) collective-permute-start(bf16[1,8,4096]{2,1,0:T(8,128)(2,1)} %refs_0_.1), channel_id=1, source_target_pairs={{0,8},{4,12},{8,0},{12,4},{1,9},{5,13},{9,1},{13,5},{2,10},{6,14},... | collective-permute-start | bytes 196616 | tf_op jit(solution)/shard_map/ppermute | solution.py:180
  3.0 6.1 %collective-permute-start = (bf16[1,8,4096]{2,1,0:T(8,128)(2,1)}, bf16[1,8,4096]{2,1,0:T(8,128)(2,1)S(1)}, u32[]{:S(2)}, u32[]{:S(2)}) collective-permute-start(bf16[1,8,4096]{2,1,0:T(8,128)(2,1)} %refs_0_.1), channel_id=1, source_target_pairs={{0,4},{4,8},{8,12},{12,0},{1,5},{5,9},{9,13},{13,1},{2,6},{6,10},{... | collective-permute-start | bytes 196616 | tf_op jit(solution)/shard_map/ppermute | solution.py:180
  3.0 6.1 %collective-permute-start.2 = (bf16[1,8,4096]{2,1,0:T(8,128)(2,1)}, bf16[1,8,4096]{2,1,0:T(8,128)(2,1)S(1)}, u32[]{:S(2)}, u32[]{:S(2)}) collective-permute-start(bf16[1,8,4096]{2,1,0:T(8,128)(2,1)} %refs_0_.1), channel_id=1, source_target_pairs={{0,12},{4,0},{8,4},{12,8},{1,13},{5,1},{9,5},{13,9},{2,14},{6,2},{... | collective-permute-start | bytes 196616 | tf_op jit(solution)/shard_map/ppermute | solution.py:180
  4.8 1.4 %copy-start.5 = (s32[113]{0:T(128)S(1)}, s32[113]{0:T(128)}, u32[]{:S(2)}) copy-start(s32[113]{0:T(128)} %starts.1) | copy-start | bytes 1360
  9.1 10.5 %slice-start = ((s8[14680064]{0:T(1024)(128)(4,1)}), s8[4194304]{0:T(1024)(128)(4,1)S(1)}, s32[]{:S(2)}) async-start(s8[14680064]{0:T(1024)(128)(4,1)} %bitcast.2), calls=%async_computation | async-start | bytes 8388608
  10.5 9.2 %collective-permute-start.3 = (bf16[32,256]{1,0:T(8,128)(2,1)S(1)}, bf16[32,256]{1,0:T(8,128)(2,1)S(1)}, u32[]{:S(2)}, u32[]{:S(2)}) collective-permute-start(bf16[32,256]{1,0:T(8,128)(2,1)S(1)} %get-tuple-element.23), channel_id=1, source_target_pairs={{0,4},{4,8},{8,12},{1,5},{5,9},{9,13},{2,6},{6,10},{10,14},{3,7},{... | collective-permute-start | bytes 49160 | tf_op jit(solution)/shard_map/ppermute | solution.py:212
  11.9 7.7 %collective-permute-start.4 = (bf16[32,256]{1,0:T(8,128)(2,1)S(1)}, bf16[32,256]{1,0:T(8,128)(2,1)S(1)}, u32[]{:S(2)}, u32[]{:S(2)}) collective-permute-start(bf16[32,256]{1,0:T(8,128)(2,1)S(1)} %get-tuple-element.24), channel_id=1, source_target_pairs={{4,0},{8,4},{12,8},{5,1},{9,5},{13,9},{6,2},{10,6},{14,10},{7,3},{... | collective-permute-start | bytes 49160 | tf_op jit(solution)/shard_map/ppermute | solution.py:211
  13.2 6.4 %slice-start.1 = ((s8[14680064]{0:T(1024)(128)(4,1)}), s8[4194304]{0:T(1024)(128)(4,1)S(1)}, s32[]{:S(2)}) async-start(s8[14680064]{0:T(1024)(128)(4,1)} %bitcast.2), calls=%async_computation.1 | async-start | bytes 8388608
  13.2 6.4 %slice-start.2 = ((s8[14680064]{0:T(1024)(128)(4,1)}), s8[4194304]{0:T(1024)(128)(4,1)S(1)}, s32[]{:S(2)}) async-start(s8[14680064]{0:T(1024)(128)(4,1)} %bitcast.2), calls=%async_computation.2 | async-start | bytes 8388608
  13.3 6.4 %slice-start.3 = ((s8[14680064]{0:T(1024)(128)(4,1)}), s8[2097152]{0:T(1024)(128)(4,1)S(1)}, s32[]{:S(2)}) async-start(s8[14680064]{0:T(1024)(128)(4,1)} %bitcast.2), calls=%async_computation.3 | async-start | bytes 4194304
  13.3 6.4 %copy-start.4 = (s32[448]{0:T(512)S(1)}, s32[448]{0:T(512)}, u32[]{:S(2)}) copy-start(s32[448]{0:T(512)} %cols.5) | copy-start | bytes 5380
  22.8 5.0 %collective-permute-start.5 = (bf16[32,1024]{1,0:T(8,128)(2,1)S(1)}, bf16[32,1024]{1,0:T(8,128)(2,1)S(1)}, u32[]{:S(2)}, u32[]{:S(2)}) collective-permute-start(bf16[32,1024]{1,0:T(8,128)(2,1)S(1)} %get-tuple-element.26), channel_id=1, source_target_pairs={{0,4},{4,8},{8,12},{12,0},{1,5},{5,9},{9,13},{13,1},{2,6},{6,10},{... | collective-permute-start | bytes 196616 | tf_op jit(solution)/shard_map/ppermute | solution.py:180
  24.8 4.3 %collective-permute-start.6 = (bf16[32,1024]{1,0:T(8,128)(2,1)S(1)}, bf16[32,1024]{1,0:T(8,128)(2,1)S(1)}, u32[]{:S(2)}, u32[]{:S(2)}) collective-permute-start(bf16[32,1024]{1,0:T(8,128)(2,1)S(1)} %get-tuple-element.27), channel_id=1, source_target_pairs={{0,8},{4,12},{8,0},{12,4},{1,9},{5,13},{9,1},{13,5},{2,10},{6,14},... | collective-permute-start | bytes 196616 | tf_op jit(solution)/shard_map/ppermute | solution.py:180
  26.5 3.3 %collective-permute-start.7 = (bf16[32,1024]{1,0:T(8,128)(2,1)S(1)}, bf16[32,1024]{1,0:T(8,128)(2,1)S(1)}, u32[]{:S(2)}, u32[]{:S(2)}) collective-permute-start(bf16[32,1024]{1,0:T(8,128)(2,1)S(1)} %get-tuple-element.28), channel_id=1, source_target_pairs={{0,12},{4,0},{8,4},{12,8},{1,13},{5,1},{9,5},{13,9},{2,14},{6,2},{... | collective-permute-start | bytes 196616 | tf_op jit(solution)/shard_map/ppermute | solution.py:180

commit v2 on v1

--- a/solution.py
+++ b/solution.py
@@ -70,19 +70,21 @@
 
 
 def edge_kernel(slots, cols, *refs):
-    pieces, (edge_gate, edge_up, by_col, to_prev, to_next, whole) = refs[:-6], refs[-6:]
+    pieces, (edge_gate, edge_up, by_col, to_inner, to_outer, whole) = refs[:-6], refs[-6:]
     size = len(pieces)
     count = cols.shape[0]
     col_blocks, rows = by_col.shape[0] - 1, by_col.shape[1]
     me = lax.axis_index("weight")
-    for step, piece in enumerate(pieces):
-        whole[lax.rem(me + size - step, size)] = piece[0]
+    for distance, piece in enumerate(pieces):
+        whole[lax.bitwise_xor(me, distance)] = piece[0]
     merged = whole[...].reshape(rows, col_blocks * 128)
     for c in range(col_blocks):
         by_col[c] = merged[:, c * 128 : (c + 1) * 128]
     by_col[col_blocks] = jnp.zeros((rows, 128), BF16)
     last_flag = slots.shape[0] - 1
-    for side, first, sent in ((0, 0, to_prev), (1, count - EDGE, to_next)):
+    is_odd = (me & 1) == 1
+    parts = []
+    for side, first in ((0, 0), (1, count - EDGE)):
         mine = slot_of(slots, 0 if side == 0 else count - 1)
         picked = []
         for q in range(EDGE):
@@ -92,7 +94,9 @@
             [edge_gate[side].reshape(EDGE * 128, 128), edge_up[side].reshape(EDGE * 128, 128)], axis=1
         )
         total = jnp.dot(jnp.concatenate(picked, axis=1), weights, preferred_element_type=F32)
-        sent[...] = jnp.where(slots[last_flag, side] == 1, total, 0.0).astype(BF16)
+        parts.append(jnp.where(slots[last_flag, side] == 1, total, 0.0).astype(BF16))
+    to_inner[...] = jnp.where(is_odd, parts[0], parts[1])
+    to_outer[...] = jnp.where(is_odd, parts[1], parts[0])
 
 
 def silu_gate(sums):
@@ -131,15 +135,18 @@
     edges[1] = sums[slot_of(slots, count - 1)]
 
 
-def down_kernel(slots, cols, hidden, edges, from_prev, from_next, down, *refs, unroll):
+def down_kernel(slots, cols, hidden, edges, from_inner, from_outer, down, *refs, unroll):
     outs, (rows_in, sums) = refs[:-2], refs[-2:]
     size = len(outs)
     count = cols.shape[0]
     rows = hidden.shape[1]
     col_blocks = sums.shape[1]
     rows_in[...] = hidden[...]
-    rows_in[0] = silu_gate(edges[0] + from_prev[...].astype(F32))
-    rows_in[slot_of(slots, count - 1)] = silu_gate(edges[1] + from_next[...].astype(F32))
+    me = lax.axis_index("weight")
+    is_odd = (me & 1) == 1
+    inner, outer = from_inner[...].astype(F32), from_outer[...].astype(F32)
+    rows_in[0] = silu_gate(edges[0] + jnp.where(is_odd, inner, outer))
+    rows_in[slot_of(slots, count - 1)] = silu_gate(edges[1] + jnp.where(is_odd, outer, inner))
     sums[...] = jnp.zeros_like(sums)
 
     def step(it, carry):
@@ -158,10 +165,9 @@
         return carry
 
     lax.fori_loop(0, count // GROUP // unroll, step, 0)
-    me = lax.axis_index("weight")
     share = col_blocks // size
     for distance, out in enumerate(outs):
-        first = lax.rem(me + distance, size) * share
+        first = lax.bitwise_xor(me, distance) * share
         for c in range(share):
             total = sums[0, first + c] + sums[1, first + c]
             out[:, c * 128 : (c + 1) * 128] = total.astype(out.dtype)
@@ -176,10 +182,12 @@
     rows = size * slab
     row_slots = (count - 1) // GROUP + 3
 
-    def shift(value, distance):
-        return lax.ppermute(value, "weight", [(d, (d + distance) % size) for d in range(size)])
-
-    pieces = [tokens] + [shift(tokens, distance) for distance in range(1, size)]
+    def swap(value, distance):
+        return lax.ppermute(value, "weight", [(d, d ^ distance) for d in range(size)])
+
+    order = list(range(2, size)) + [1]
+    arrived = {distance: swap(tokens, distance) for distance in order}
+    pieces = [tokens] + [arrived[distance] for distance in range(1, size)]
     slot_rows = -(-count // 128) + 1
     slots, edge_gate, edge_up = pl.pallas_call(
         functools.partial(prepare_kernel, count=count),
@@ -195,7 +203,7 @@
         cost_estimate=cost(2**36),
         name="prepare",
     )(row_starts, in_hbm(gate_blocks), in_hbm(up_blocks))
-    by_col, to_prev, to_next = pl.pallas_call(
+    by_col, to_inner, to_outer = pl.pallas_call(
         edge_kernel,
         out_shape=(
             pltpu.VMEM((col_blocks + 1, rows, width), BF16),
@@ -208,8 +216,9 @@
         compiler_params=limit(4),
         name="edges",
     )(slots, gate_cols, *pieces, edge_gate, edge_up)
-    from_next = lax.ppermute(to_prev, "weight", [(d + 1, d) for d in range(size - 1)])
-    from_prev = lax.ppermute(to_next, "weight", [(d, d + 1) for d in range(size - 1)])
+    outer_pairs = [(d, (d + 1 if d % 2 else d - 1) % size) for d in range(size)]
+    from_outer = lax.ppermute(to_outer, "weight", outer_pairs)
+    from_inner = swap(to_inner, 1)
     hidden, edges = pl.pallas_call(
         functools.partial(hidden_kernel, unroll=largest_unroll(count // GROUP, 28)),
         out_shape=(
@@ -237,10 +246,11 @@
         ],
         compiler_params=limit(8),
         name="down",
-    )(slots, down_cols, hidden, edges, from_prev, from_next, in_vmem(down_blocks))
+    )(slots, down_cols, hidden, edges, from_inner, from_outer, in_vmem(down_blocks))
+    received = {distance: swap(outs[distance], distance) for distance in order}
     total = outs[0]
-    for distance in range(1, size):
-        total = total + shift(outs[distance], distance).astype(F32)
+    for distance in order:
+        total = total + received[distance].astype(F32)
     return total.astype(BF16).reshape(size, slab, model_width // size)
 
 

time: 30.7 us -> 28.7 us (0.935)
  starting transfers between devices: 12.5 us -> 8.27 us
  waiting for transfers between devices: 1.92 us -> 3.95 us
    ppermute x8, starting transfers between devices: 12.5 us -> 8.27 us  [the longest x7 6.48 us: swap(): lax.ppermute(value, 'weight', [(d, d ^ distance) for d in range(size)])]
    ppermute x8, waiting for transfers between devices: 1.92 us -> 3.95 us  [the longest x7 3.95 us: swap(): lax.ppermute(value, 'weight', [(d, d ^ distance) for d in range(size)])]
  transfers between devices with their start and end apart: 8 -> 8, of which waited for: 2 -> 2; matrix products, arithmetic and copies ran while one was open for 0% -> 0% of each run, Pallas kernels for 30% -> 33%
where the time goes in v2:
time: 28.7 us; the launch traced here: 28.5 us
  Pallas kernels  14 us (49%)
  starting transfers between devices  8.27 us (29%)
  waiting for transfers between devices  3.95 us (14%)
  local copies, waits for them, and re-layouts  1.48 us (5%)
  other arithmetic  0.66 us (2%)
    ppermute x7, starting transfers between devices, swap(): lax.ppermute(value, 'weight', [(d, d ^ distance) for d in range(size)])  6.48 us
    pallas_call x1, Pallas kernels, per_device(): pl.pallas_call(functools.partial(hidden_kernel, unroll=largest_unroll(cou...  6.35 us
    ppermute x7, waiting for transfers between devices, swap(): lax.ppermute(value, 'weight', [(d, d ^ distance) for d in range(size)])  3.95 us
    pallas_call x1, Pallas kernels, per_device(): pl.pallas_call(functools.partial(prepare_kernel, count=count), out_shape=...  3.17 us
    pallas_call x1, Pallas kernels, per_device(): pl.pallas_call(functools.partial(down_kernel, unroll=largest_unroll(count...  3.11 us
    ppermute x1, starting transfers between devices, per_device(): from_outer = lax.ppermute(to_outer, 'weight', outer_pairs)  1.79 us
    unnamed x20, local copies, waits for them, and re-layouts  1.48 us
    pallas_call x1, Pallas kernels, per_device(): pl.pallas_call(edge_kernel, out_shape=(pltpu.VMEM((col_blocks + 1, rows,...  1.35 us
  transfers between devices with their start and end apart: 8, of which 2 were waited for; matrix products, arithmetic and copies ran while one was open for 0% of the time, Pallas kernels for 33%

profile of v2, /device:TPU:0, one launch (start us, length us, event | category | flops | bytes accessed | tf_op | source)
XLA Modules:
  0.0 28.5 jit_solution(7627892258373448640)
XLA Ops:
  0.0 0.0 copy-start.2
  0.0 0.0 copy-start.1
  0.0 0.0 copy-start
  0.0 0.0 copy-start.3
  0.0 3.0 %collective-permute-start.1 = (bf16[1,8,4096]{2,1,0:T(8,128)(2,1)}, bf16[1,8,4096]{2,1,0:T(8,128)(2,1)S(1)}, u32[]{:S(2)}, u32[]{:S(2)}) collective-permute-start(bf16[1,8,4096]{2,1,0:T(8,128)(2,1)} %refs_0_.1), channel_id=1, source_target_pairs={{0,8},{4,12},{8,0},{12,4},{1,9},{5,13},{9,1},{13,5},{2,10},{6,14},... | collective-permute-start | bytes 196616 | tf_op jit(solution)/shard_map/ppermute | solution.py:186
  3.0 0.0 collective-permute-start
  3.0 0.2 collective-permute-start.2
  3.2 0.0 copy-start.5
  3.2 1.4 %copy-done.5 = s32[113]{0:T(128)S(1)} copy-done((s32[113]{0:T(128)S(1)}, s32[113]{0:T(128)}, u32[]{:S(2)}) %copy-start.5) | copy-done | bytes 476
  4.7 3.2 %prepare.1 = (s32[5,128]{1,0:T(8,128)S(1)}, bf16[2,24,128,128]{3,2,1,0:T(8,128)(2,1)S(1)}, bf16[2,24,128,128]{3,2,1,0:T(8,128)(2,1)S(1)}) custom-call(s32[113]{0:T(128)S(1)} %copy-done.5, bf16[448,128,128]{2,1,0:T(8,128)(2,1)} %gate.3, bf16[448,128,128]{2,1,0:T(8,128)(2,1)} %up.3), custom_call_target="tpu_custom_call" | custom-call | flops 68719476736 | bytes 1048576 | tf_op jit(solution)/shard_map/prepare/pallas_call | solution.py:192
  7.8 0.0 collective-permute-done.1.refs_2_
  7.9 0.0 collective-permute-done.refs_1_
  7.9 0.0 collective-permute-done.2.refs_3_
  7.9 0.0 copy-done.2
  7.9 0.0 copy-done.3
  7.9 0.0 slice-start
  7.9 1.3 %edges.1 = (bf16[33,32,128]{2,1,0:T(8,128)(2,1)S(1)}, bf16[32,256]{1,0:T(8,128)(2,1)S(1)}, bf16[32,256]{1,0:T(8,128)(2,1)S(1)}) custom-call(s32[5,128]{1,0:T(8,128)S(1)} %get-tuple-element.17.slots, s32[448]{0:T(512)S(1)} %copy-done.3, bf16[1,8,4096]{2,1,0:T(8,128)(2,1)S(1)} %copy-done.2, bf16[1,8,4096]{2,1,0:T(8,128)(2,1)S(1)} %collective-permute-done.refs_1_, ...), custom_call_target="tpu_custom_call" | custom-call | tf_op jit(solution)/shard_map/edges/pallas_call | solution.py:206
  9.3 0.4 %collective-permute-start.3 = (bf16[32,256]{1,0:T(8,128)(2,1)S(1)}, bf16[32,256]{1,0:T(8,128)(2,1)S(1)}, u32[]{:S(2)}, u32[]{:S(2)}) collective-permute-start(bf16[32,256]{1,0:T(8,128)(2,1)S(1)} %get-tuple-element.23), channel_id=1, source_target_pairs={{0,4},{4,0},{8,12},{12,8},{1,5},{5,1},{9,13},{13,9},{2,6},{6,2},{1... | collective-permute-start | bytes 49160 | tf_op jit(solution)/shard_map/ppermute | solution.py:186
  9.6 1.8 %collective-permute-start.4 = (bf16[32,256]{1,0:T(8,128)(2,1)S(1)}, bf16[32,256]{1,0:T(8,128)(2,1)S(1)}, u32[]{:S(2)}, u32[]{:S(2)}) collective-permute-start(bf16[32,256]{1,0:T(8,128)(2,1)S(1)} %get-tuple-element.24), channel_id=1, source_target_pairs={{0,12},{4,8},{8,4},{12,0},{1,13},{5,9},{9,5},{13,1},{2,14},{6,10},... | collective-permute-start | bytes 49160 | tf_op jit(solution)/shard_map/ppermute | solution.py:220
  11.4 0.0 copy-done.1
  11.4 0.0 copy-done
  11.4 0.0 slice-start.1
  11.4 0.0 slice-start.2
  11.4 0.0 slice-start.3
  11.5 0.0 copy-start.4
  11.5 6.3 %hidden.1 = (bf16[58,32,128]{2,1,0:T(8,128)(2,1)S(1)}, f32[2,32,256]{2,1,0:T(8,128)S(1)}) custom-call(s32[5,128]{1,0:T(8,128)S(1)} %get-tuple-element.17.slots, s32[448]{0:T(512)S(1)} %copy-done.3, bf16[33,32,128]{2,1,0:T(8,128)(2,1)S(1)} %get-tuple-element.20.by_col, bf16[448,128,128]{2,1,0:T(8,128)(2,1)S(1)} %copy-done, bf16[448,128,128]{2,1,0:T(8,128)(2,1)S(1)} %copy-done.1), custom_call_target="tpu_custom_call" | custom-call | flops 1073741824 | bytes 1048576 | tf_op jit(solution)/shard_map/hidden/pallas_call | solution.py:222
  17.8 0.0 collective-permute-done.3.from_inner
  17.8 0.0 collective-permute-done.4.from_outer
  17.8 0.0 slice-done
  17.9 0.0 slice-done.1
  17.9 0.0 slice-done.2
  17.9 0.0 slice-done.3
  17.9 0.0 copy-done.4
  17.9 3.1 %down.2 = (f32[32,1024]{1,0:T(8,128)S(1)}, bf16[32,1024]{1,0:T(8,128)(2,1)S(1)}, bf16[32,1024]{1,0:T(8,128)(2,1)S(1)}, bf16[32,1024]{1,0:T(8,128)(2,1)S(1)}) custom-call(s32[5,128]{1,0:T(8,128)S(1)} %get-tuple-element.17.slots, s32[448]{0:T(512)S(1)} %copy-done.4, bf16[58,32,128]{2,1,0:T(8,128)(2,1)S(1)} %get-tuple-element.21.hidden, ...), custom_call_target="tpu_custom_call" | custom-call | tf_op jit(solution)/shard_map/down/pallas_call | solution.py:235
  21.0 2.7 %collective-permute-start.5 = (bf16[32,1024]{1,0:T(8,128)(2,1)S(1)}, bf16[32,1024]{1,0:T(8,128)(2,1)S(1)}, u32[]{:S(2)}, u32[]{:S(2)}) collective-permute-start(bf16[32,1024]{1,0:T(8,128)(2,1)S(1)} %get-tuple-element.26), channel_id=1, source_target_pairs={{0,8},{4,12},{8,0},{12,4},{1,9},{5,13},{9,1},{13,5},{2,10},{6,14},... | collective-permute-start | bytes 196616 | tf_op jit(solution)/shard_map/ppermute | solution.py:186
  23.7 0.0 collective-permute-start.6
  23.7 0.2 collective-permute-start.7
  23.9 2.1 %collective-permute-done.5 = bf16[32,1024]{1,0:T(8,128)(2,1)S(1)} collective-permute-done((bf16[32,1024]{1,0:T(8,128)(2,1)S(1)}, bf16[32,1024]{1,0:T(8,128)(2,1)S(1)}, u32[]{:S(2)}, u32[]{:S(2)}) %collective-permute-start.5) | collective-permute-done | bytes 65568 | tf_op jit(solution)/shard_map/ppermute | solution.py:186
  26.0 1.9 %collective-permute-done.6 = bf16[32,1024]{1,0:T(8,128)(2,1)S(1)} collective-permute-done((bf16[32,1024]{1,0:T(8,128)(2,1)S(1)}, bf16[32,1024]{1,0:T(8,128)(2,1)S(1)}, u32[]{:S(2)}, u32[]{:S(2)}) %collective-permute-start.6) | collective-permute-done | bytes 65568 | tf_op jit(solution)/shard_map/ppermute | solution.py:186
  27.8 0.0 collective-permute-done.7
  27.8 0.7 %fusion = bf16[4,8,1024]{2,1,0:T(8,128)(2,1)} fusion(bf16[32,1024]{1,0:T(8,128)(2,1)S(1)} %collective-permute-done.7, bf16[32,1024]{1,0:T(8,128)(2,1)S(1)} %collective-permute-done.6, f32[32,1024]{1,0:T(8,128)S(1)} %get-tuple-element.25, bf16[32,1024]{1,0:T(8,128)(2,1)S(1)} %collective-permute-done.5), kind=kLoop, calls=%fused_computation.1 | loop fusion | flops 229376 | bytes 393216 | tf_op jit(solution)/shard_map/reshape | solution.py:254
  (1 shorter events, 0.0 us)
Async XLA Ops:
  0.0 7.9 %copy-start.2 = (bf16[1,8,4096]{2,1,0:T(8,128)(2,1)S(1)}, bf16[1,8,4096]{2,1,0:T(8,128)(2,1)}, u32[]{:S(2)}) copy-start(bf16[1,8,4096]{2,1,0:T(8,128)(2,1)} %refs_0_.1) | copy-start | bytes 196612
  0.0 11.4 %copy-start.1 = (bf16[448,128,128]{2,1,0:T(8,128)(2,1)S(1)}, bf16[448,128,128]{2,1,0:T(8,128)(2,1)}, u32[]{:S(2)}) copy-start(bf16[448,128,128]{2,1,0:T(8,128)(2,1)} %up.3) | copy-start | bytes 44040196
  0.0 11.4 %copy-start = (bf16[448,128,128]{2,1,0:T(8,128)(2,1)S(1)}, bf16[448,128,128]{2,1,0:T(8,128)(2,1)}, u32[]{:S(2)}) copy-start(bf16[448,128,128]{2,1,0:T(8,128)(2,1)} %gate.3) | copy-start | bytes 44040196
  0.0 7.9 %copy-start.3 = (s32[448]{0:T(512)S(1)}, s32[448]{0:T(512)}, u32[]{:S(2)}) copy-start(s32[448]{0:T(512)} %cols.4) | copy-start | bytes 5380
  0.0 7.8 %collective-permute-start.1 = (bf16[1,8,4096]{2,1,0:T(8,128)(2,1)}, bf16[1,8,4096]{2,1,0:T(8,128)(2,1)S(1)}, u32[]{:S(2)}, u32[]{:S(2)}) collective-permute-start(bf16[1,8,4096]{2,1,0:T(8,128)(2,1)} %refs_0_.1), channel_id=1, source_target_pairs={{0,8},{4,12},{8,0},{12,4},{1,9},{5,13},{9,1},{13,5},{2,10},{6,14},... | collective-permute-start | bytes 196616 | tf_op jit(solution)/shard_map/ppermute | solution.py:186
  3.0 4.8 %collective-permute-start = (bf16[1,8,4096]{2,1,0:T(8,128)(2,1)}, bf16[1,8,4096]{2,1,0:T(8,128)(2,1)S(1)}, u32[]{:S(2)}, u32[]{:S(2)}) collective-permute-start(bf16[1,8,4096]{2,1,0:T(8,128)(2,1)} %refs_0_.1), channel_id=1, source_target_pairs={{0,4},{4,0},{8,12},{12,8},{1,5},{5,1},{9,13},{13,9},{2,6},{6,2},{1... | collective-permute-start | bytes 196616 | tf_op jit(solution)/shard_map/ppermute | solution.py:186
  3.0 4.8 %collective-permute-start.2 = (bf16[1,8,4096]{2,1,0:T(8,128)(2,1)}, bf16[1,8,4096]{2,1,0:T(8,128)(2,1)S(1)}, u32[]{:S(2)}, u32[]{:S(2)}) collective-permute-start(bf16[1,8,4096]{2,1,0:T(8,128)(2,1)} %refs_0_.1), channel_id=1, source_target_pairs={{0,12},{4,8},{8,4},{12,0},{1,13},{5,9},{9,5},{13,1},{2,14},{6,10},... | collective-permute-start | bytes 196616 | tf_op jit(solution)/shard_map/ppermute | solution.py:186
  3.2 1.4 %copy-start.5 = (s32[113]{0:T(128)S(1)}, s32[113]{0:T(128)}, u32[]{:S(2)}) copy-start(s32[113]{0:T(128)} %starts.1) | copy-start | bytes 1360
  7.9 9.9 %slice-start = ((s8[14680064]{0:T(1024)(128)(4,1)}), s8[4194304]{0:T(1024)(128)(4,1)S(1)}, s32[]{:S(2)}) async-start(s8[14680064]{0:T(1024)(128)(4,1)} %bitcast.2), calls=%async_computation | async-start | bytes 8388608
  9.3 8.6 %collective-permute-start.3 = (bf16[32,256]{1,0:T(8,128)(2,1)S(1)}, bf16[32,256]{1,0:T(8,128)(2,1)S(1)}, u32[]{:S(2)}, u32[]{:S(2)}) collective-permute-start(bf16[32,256]{1,0:T(8,128)(2,1)S(1)} %get-tuple-element.23), channel_id=1, source_target_pairs={{0,4},{4,0},{8,12},{12,8},{1,5},{5,1},{9,13},{13,9},{2,6},{6,2},{1... | collective-permute-start | bytes 49160 | tf_op jit(solution)/shard_map/ppermute | solution.py:186
  9.6 8.2 %collective-permute-start.4 = (bf16[32,256]{1,0:T(8,128)(2,1)S(1)}, bf16[32,256]{1,0:T(8,128)(2,1)S(1)}, u32[]{:S(2)}, u32[]{:S(2)}) collective-permute-start(bf16[32,256]{1,0:T(8,128)(2,1)S(1)} %get-tuple-element.24), channel_id=1, source_target_pairs={{0,12},{4,8},{8,4},{12,0},{1,13},{5,9},{9,5},{13,1},{2,14},{6,10},... | collective-permute-start | bytes 49160 | tf_op jit(solution)/shard_map/ppermute | solution.py:220
  11.4 6.4 %slice-start.1 = ((s8[14680064]{0:T(1024)(128)(4,1)}), s8[4194304]{0:T(1024)(128)(4,1)S(1)}, s32[]{:S(2)}) async-start(s8[14680064]{0:T(1024)(128)(4,1)} %bitcast.2), calls=%async_computation.1 | async-start | bytes 8388608
  11.4 6.4 %slice-start.2 = ((s8[14680064]{0:T(1024)(128)(4,1)}), s8[4194304]{0:T(1024)(128)(4,1)S(1)}, s32[]{:S(2)}) async-start(s8[14680064]{0:T(1024)(128)(4,1)} %bitcast.2), calls=%async_computation.2 | async-start | bytes 8388608
  11.4 6.4 %slice-start.3 = ((s8[14680064]{0:T(1024)(128)(4,1)}), s8[2097152]{0:T(1024)(128)(4,1)S(1)}, s32[]{:S(2)}) async-start(s8[14680064]{0:T(1024)(128)(4,1)} %bitcast.2), calls=%async_computation.3 | async-start | bytes 4194304
  11.5 6.4 %copy-start.4 = (s32[448]{0:T(512)S(1)}, s32[448]{0:T(512)}, u32[]{:S(2)}) copy-start(s32[448]{0:T(512)} %cols.5) | copy-start | bytes 5380
  21.0 4.9 %collective-permute-start.5 = (bf16[32,1024]{1,0:T(8,128)(2,1)S(1)}, bf16[32,1024]{1,0:T(8,128)(2,1)S(1)}, u32[]{:S(2)}, u32[]{:S(2)}) collective-permute-start(bf16[32,1024]{1,0:T(8,128)(2,1)S(1)} %get-tuple-element.26), channel_id=1, source_target_pairs={{0,8},{4,12},{8,0},{12,4},{1,9},{5,13},{9,1},{13,5},{2,10},{6,14},... | collective-permute-start | bytes 196616 | tf_op jit(solution)/shard_map/ppermute | solution.py:186
  23.7 4.1 %collective-permute-start.6 = (bf16[32,1024]{1,0:T(8,128)(2,1)S(1)}, bf16[32,1024]{1,0:T(8,128)(2,1)S(1)}, u32[]{:S(2)}, u32[]{:S(2)}) collective-permute-start(bf16[32,1024]{1,0:T(8,128)(2,1)S(1)} %get-tuple-element.27), channel_id=1, source_target_pairs={{0,12},{4,8},{8,4},{12,0},{1,13},{5,9},{9,5},{13,1},{2,14},{6,10},... | collective-permute-start | bytes 196616 | tf_op jit(solution)/shard_map/ppermute | solution.py:186
  23.7 4.1 %collective-permute-start.7 = (bf16[32,1024]{1,0:T(8,128)(2,1)S(1)}, bf16[32,1024]{1,0:T(8,128)(2,1)S(1)}, u32[]{:S(2)}, u32[]{:S(2)}) collective-permute-start(bf16[32,1024]{1,0:T(8,128)(2,1)S(1)} %get-tuple-element.28), channel_id=1, source_target_pairs={{0,4},{4,0},{8,12},{12,8},{1,5},{5,1},{9,13},{13,9},{2,6},{6,2},{1... | collective-permute-start | bytes 196616 | tf_op jit(solution)/shard_map/ppermute | solution.py:186

commit v3 on v2

--- a/solution.py
+++ b/solution.py
@@ -21,10 +21,10 @@
 
 
 def cost(flops):
-    return pl.CostEstimate(flops=flops, bytes_accessed=2**20, transcendentals=0)
-
-
-def largest_unroll(steps, most):
+    return pl.CostEstimate(flops=flops, bytes_accessed=2**10, transcendentals=0)
+
+
+def largest_divisor(steps, most):
     return max(u for u in range(1, most + 1) if steps % u == 0)
 
 
@@ -36,13 +36,10 @@
     return pltpu.with_memory_space_constraint(value, pltpu.HBM)
 
 
-def prepare_kernel(starts, gate, up, slots, edge_gate, edge_up, sems, *, count):
-    copies = []
-    for k, (source, target) in enumerate(((gate, edge_gate), (up, edge_up))):
-        for side, first in enumerate((0, count - EDGE)):
-            copies.append(
-                pltpu.make_async_copy(source.at[pl.ds(first, EDGE)], target.at[side], sems.at[k, side])
-            )
+def prepare_kernel(starts, up, slots, edge_up, smem_starts, sems, *, count):
+    copies = [pltpu.make_async_copy(starts, smem_starts, sems.at[2])]
+    for side, first in enumerate((0, count - EDGE)):
+        copies.append(pltpu.make_async_copy(up.at[pl.ds(first, EDGE)], edge_up.at[side], sems.at[side]))
     for copy in copies:
         copy.start()
     first_block = lax.axis_index("weight") * count
@@ -50,8 +47,9 @@
     place = first_block + lax.broadcasted_iota(jnp.int32, slots.shape, 0) * 128 + lanes
     row = jnp.zeros(slots.shape, jnp.int32)
     first_row, enters, leaves = 0, 1, 1
-    for f in range(1, starts.shape[0]):
-        start = starts[f]
+    copies[0].wait()
+    for f in range(1, smem_starts.shape[0]):
+        start = smem_starts[f]
         row += (start <= place).astype(jnp.int32)
         first_row += (start <= first_block).astype(jnp.int32)
         enters = jnp.where(start == first_block, 0, enters)
@@ -59,7 +57,7 @@
     enters = jnp.where(first_block == 0, 0, enters)
     flag_row = lax.broadcasted_iota(jnp.int32, slots.shape, 0) == slots.shape[0] - 1
     slots[...] = jnp.where(flag_row, jnp.where(lanes == 0, enters, leaves), row - first_row)
-    for copy in copies:
+    for copy in copies[1:]:
         copy.wait()
 
 
@@ -70,7 +68,7 @@
 
 
 def edge_kernel(slots, cols, *refs):
-    pieces, (edge_gate, edge_up, by_col, to_inner, to_outer, whole) = refs[:-6], refs[-6:]
+    pieces, (gate, edge_up, by_col, to_inner, to_outer, whole) = refs[:-6], refs[-6:]
     size = len(pieces)
     count = cols.shape[0]
     col_blocks, rows = by_col.shape[0] - 1, by_col.shape[1]
@@ -91,7 +89,7 @@
             block = first + q
             picked.append(by_col[jnp.where(slot_of(slots, block) == mine, cols[block], col_blocks)])
         weights = jnp.concatenate(
-            [edge_gate[side].reshape(EDGE * 128, 128), edge_up[side].reshape(EDGE * 128, 128)], axis=1
+            [gate[first : first + EDGE].reshape(EDGE * 128, 128), edge_up[side].reshape(EDGE * 128, 128)], axis=1
         )
         total = jnp.dot(jnp.concatenate(picked, axis=1), weights, preferred_element_type=F32)
         parts.append(jnp.where(slots[last_flag, side] == 1, total, 0.0).astype(BF16))
@@ -99,12 +97,11 @@
     to_outer[...] = jnp.where(is_odd, parts[1], parts[0])
 
 
-def silu_gate(sums):
-    gate, up = sums[..., :128], sums[..., 128:]
+def silu_gate(gate, up):
     return (gate / (1 + jnp.exp(-gate)) * up).astype(BF16)
 
 
-def hidden_kernel(slots, cols, by_col, gate, up, hidden, edges, sums, *, unroll):
+def add_rows(slots, cols, by_col, weights, sums, unroll):
     col_blocks, rows = by_col.shape[0] - 1, by_col.shape[1]
     count = cols.shape[0]
     sums[...] = jnp.zeros_like(sums)
@@ -119,9 +116,7 @@
                 even.append(by_col[jnp.where(is_odd, col_blocks, col)])
                 odd.append(by_col[jnp.where(is_odd, col, col_blocks)])
             left = jnp.concatenate([jnp.concatenate(even, axis=1), jnp.concatenate(odd, axis=1)], axis=0)
-            right = jnp.concatenate(
-                [ref[pl.ds(first, GROUP)].reshape(GROUP * 128, 128) for ref in (gate, up)], axis=1
-            )
+            right = weights[pl.ds(first, GROUP)].reshape(GROUP * 128, 128)
             part = jnp.dot(left, right, preferred_element_type=F32)
             at_even, at_odd = slot + (slot & 1), slot | 1
             old_even, old_odd = sums[at_even], sums[at_odd]
@@ -130,9 +125,18 @@
         return carry
 
     lax.fori_loop(0, count // GROUP // unroll, step, 0)
-    hidden[...] = silu_gate(sums[...])
-    edges[0] = sums[0]
-    edges[1] = sums[slot_of(slots, count - 1)]
+
+
+def gate_kernel(slots, cols, by_col, gate, sums, *, unroll):
+    add_rows(slots, cols, by_col, gate, sums, unroll)
+
+
+def up_kernel(slots, cols, by_col, up, gate_sums, hidden, edges, sums, *, unroll):
+    add_rows(slots, cols, by_col, up, sums, unroll)
+    hidden[...] = silu_gate(gate_sums[...], sums[...])
+    for side, slot in enumerate((0, slot_of(slots, cols.shape[0] - 1))):
+        edges[side, 0] = gate_sums[slot]
+        edges[side, 1] = sums[slot]
 
 
 def down_kernel(slots, cols, hidden, edges, from_inner, from_outer, down, *refs, unroll):
@@ -145,8 +149,9 @@
     me = lax.axis_index("weight")
     is_odd = (me & 1) == 1
     inner, outer = from_inner[...].astype(F32), from_outer[...].astype(F32)
-    rows_in[0] = silu_gate(edges[0] + jnp.where(is_odd, inner, outer))
-    rows_in[slot_of(slots, count - 1)] = silu_gate(edges[1] + jnp.where(is_odd, outer, inner))
+    before, after = jnp.where(is_odd, inner, outer), jnp.where(is_odd, outer, inner)
+    for side, slot, part in ((0, 0, before), (1, slot_of(slots, count - 1), after)):
+        rows_in[slot] = silu_gate(edges[side, 0] + part[:, :128], edges[side, 1] + part[:, 128:])
     sums[...] = jnp.zeros_like(sums)
 
     def step(it, carry):
@@ -189,20 +194,19 @@
     arrived = {distance: swap(tokens, distance) for distance in order}
     pieces = [tokens] + [arrived[distance] for distance in range(1, size)]
     slot_rows = -(-count // 128) + 1
-    slots, edge_gate, edge_up = pl.pallas_call(
+    slots, edge_up = pl.pallas_call(
         functools.partial(prepare_kernel, count=count),
         out_shape=(
             jax.ShapeDtypeStruct((slot_rows, 128), jnp.int32),
             pltpu.VMEM((2, EDGE, width, width), BF16),
-            pltpu.VMEM((2, EDGE, width, width), BF16),
-        ),
-        in_specs=[SM, HB, HB],
-        out_specs=(VM, VM, VM),
-        scratch_shapes=[pltpu.SemaphoreType.DMA((2, 2))],
+        ),
+        in_specs=[HB, HB],
+        out_specs=(VM, VM),
+        scratch_shapes=[pltpu.SMEM(row_starts.shape, jnp.int32), pltpu.SemaphoreType.DMA((3,))],
         compiler_params=limit(4),
         cost_estimate=cost(2**36),
         name="prepare",
-    )(row_starts, in_hbm(gate_blocks), in_hbm(up_blocks))
+    )(in_hbm(row_starts), in_hbm(up_blocks))
     by_col, to_inner, to_outer = pl.pallas_call(
         edge_kernel,
         out_shape=(
@@ -214,26 +218,37 @@
         out_specs=(VM, VM, VM),
         scratch_shapes=[pltpu.VMEM((size, slab, model_width), BF16)],
         compiler_params=limit(4),
+        cost_estimate=cost(2**19),
         name="edges",
-    )(slots, gate_cols, *pieces, edge_gate, edge_up)
+    )(slots, gate_cols, *pieces, in_vmem(gate_blocks), edge_up)
     outer_pairs = [(d, (d + 1 if d % 2 else d - 1) % size) for d in range(size)]
     from_outer = lax.ppermute(to_outer, "weight", outer_pairs)
     from_inner = swap(to_inner, 1)
+    unroll = largest_divisor(count // GROUP, 28)
+    gate_sums = pl.pallas_call(
+        functools.partial(gate_kernel, unroll=unroll),
+        out_shape=pltpu.VMEM((row_slots, rows, width), F32),
+        in_specs=[SM, SM, VM, VM],
+        out_specs=VM,
+        compiler_params=limit(8),
+        cost_estimate=cost(2**20),
+        name="gate",
+    )(slots, gate_cols, by_col, in_vmem(gate_blocks))
     hidden, edges = pl.pallas_call(
-        functools.partial(hidden_kernel, unroll=largest_unroll(count // GROUP, 28)),
+        functools.partial(up_kernel, unroll=unroll),
         out_shape=(
             pltpu.VMEM((row_slots, rows, width), BF16),
-            pltpu.VMEM((2, rows, 2 * width), F32),
+            pltpu.VMEM((2, 2, rows, width), F32),
         ),
         in_specs=[SM, SM, VM, VM, VM],
         out_specs=(VM, VM),
-        scratch_shapes=[pltpu.VMEM((row_slots, rows, 2 * width), F32)],
+        scratch_shapes=[pltpu.VMEM((row_slots, rows, width), F32)],
         compiler_params=limit(8),
-        cost_estimate=cost(2**30),
-        name="hidden",
-    )(slots, gate_cols, by_col, in_vmem(gate_blocks), in_vmem(up_blocks))
+        cost_estimate=cost(2**33),
+        name="up",
+    )(slots, gate_cols, by_col, in_vmem(up_blocks), in_vmem(gate_sums))
     outs = pl.pallas_call(
-        functools.partial(down_kernel, unroll=largest_unroll(count // GROUP, 28)),
+        functools.partial(down_kernel, unroll=unroll),
         out_shape=tuple(
             jax.ShapeDtypeStruct((rows, model_width // size), BF16 if distance else F32)
             for distance in range(size)
@@ -245,6 +260,7 @@
             pltpu.VMEM((2, col_blocks, rows, width), F32),
         ],
         compiler_params=limit(8),
+        cost_estimate=cost(2**18),
         name="down",
     )(slots, down_cols, hidden, edges, from_inner, from_outer, in_vmem(down_blocks))
     received = {distance: swap(outs[distance], distance) for distance in order}

time: 28.7 us -> 26.6 us (0.927)
  local copies, waits for them, and re-layouts: 1.48 us -> 0.04 us
  starting transfers between devices: 8.27 us -> 7.25 us
  waiting for transfers between devices: 3.95 us -> 4.7 us
  Pallas kernels: 14 us -> 13.6 us
    unnamed x20 -> x18, local copies, waits for them, and re-layouts: 1.48 us -> 0.04 us
    pallas_call x1, Pallas kernels: 3.17 us -> 2.14 us  [per_device(): pl.pallas_call(functools.partial(prepare_kernel, count=count), out_shape=...]
    ppermute x7, waiting for transfers between devices: 3.95 us -> 4.7 us  [swap(): lax.ppermute(value, 'weight', [(d, d ^ distance) for d in range(size)])]
    pallas_call x2 -> x3, Pallas kernels: 9.45 us -> 10.2 us  [the longest x1 3.68 us: per_device(): pl.pallas_call(functools.partial(up_kernel, unroll=unroll), out_shape=(pl...]
    ppermute x7, starting transfers between devices: 6.48 us -> 5.95 us  [swap(): lax.ppermute(value, 'weight', [(d, d ^ distance) for d in range(size)])]
    ppermute x1, starting transfers between devices: 1.79 us -> 1.3 us  [per_device(): from_outer = lax.ppermute(to_outer, 'weight', outer_pairs)]
  transfers between devices with their start and end apart: 8 -> 8, of which waited for: 2 -> 4; matrix products, arithmetic and copies ran while one was open for 0% -> 0% of each run, Pallas kernels for 33% -> 35%
where the time goes in v3:
time: 26.6 us; the launch traced here: 26.5 us
  Pallas kernels  13.6 us (51%)
  starting transfers between devices  7.25 us (27%)
  waiting for transfers between devices  4.7 us (18%)
  other arithmetic  0.67 us (3%)
    ppermute x7, starting transfers between devices, swap(): lax.ppermute(value, 'weight', [(d, d ^ distance) for d in range(size)])  5.95 us
    ppermute x7, waiting for transfers between devices, swap(): lax.ppermute(value, 'weight', [(d, d ^ distance) for d in range(size)])  4.7 us
    pallas_call x1, Pallas kernels, per_device(): pl.pallas_call(functools.partial(up_kernel, unroll=unroll), out_shape=(pl...  3.68 us
    pallas_call x1, Pallas kernels, per_device(): pl.pallas_call(functools.partial(gate_kernel, unroll=unroll), out_shape=p...  3.36 us
    pallas_call x1, Pallas kernels, per_device(): pl.pallas_call(functools.partial(down_kernel, unroll=unroll), out_shape=t...  3.12 us
    pallas_call x1, Pallas kernels, per_device(): pl.pallas_call(functools.partial(prepare_kernel, count=count), out_shape=...  2.14 us
    pallas_call x1, Pallas kernels, per_device(): pl.pallas_call(edge_kernel, out_shape=(pltpu.VMEM((col_blocks + 1, rows,...  1.34 us
    ppermute x1, starting transfers between devices, per_device(): from_outer = lax.ppermute(to_outer, 'weight', outer_pairs)  1.3 us
  transfers between devices with their start and end apart: 8, of which 4 were waited for; matrix products, arithmetic and copies ran while one was open for 0% of the time, Pallas kernels for 35%

profile of v3, /device:TPU:0, one launch (start us, length us, event | category | flops | bytes accessed | tf_op | source)
XLA Modules:
  0.0 26.5 jit_solution(9618403288898503338)
XLA Ops:
  0.0 0.0 copy-start.1
  0.0 0.0 copy-start.2
  0.0 0.0 copy-start
  0.0 3.0 %collective-permute-start.1 = (bf16[1,8,4096]{2,1,0:T(8,128)(2,1)}, bf16[1,8,4096]{2,1,0:T(8,128)(2,1)S(1)}, u32[]{:S(2)}, u32[]{:S(2)}) collective-permute-start(bf16[1,8,4096]{2,1,0:T(8,128)(2,1)} %refs_0_.1), channel_id=1, source_target_pairs={{0,8},{4,12},{8,0},{12,4},{1,9},{5,13},{9,1},{13,5},{2,10},{6,14},... | collective-permute-start | bytes 196616 | tf_op jit(solution)/shard_map/ppermute | solution.py:191
  3.0 0.0 collective-permute-start
  3.0 0.2 collective-permute-start.2
  3.2 2.1 %prepare.1 = (s32[5,128]{1,0:T(8,128)S(1)}, bf16[2,24,128,128]{3,2,1,0:T(8,128)(2,1)S(1)}) custom-call(s32[113]{0:T(128)} %starts.1, bf16[448,128,128]{2,1,0:T(8,128)(2,1)} %up.5), custom_call_target="tpu_custom_call" | custom-call | flops 68719476736 | bytes 1024 | tf_op jit(solution)/shard_map/prepare/pallas_call | solution.py:197
  5.4 0.3 %collective-permute-done.1.refs_2_ = bf16[1,8,4096]{2,1,0:T(8,128)(2,1)S(1)} collective-permute-done((bf16[1,8,4096]{2,1,0:T(8,128)(2,1)}, bf16[1,8,4096]{2,1,0:T(8,128)(2,1)S(1)}, u32[]{:S(2)}, u32[]{:S(2)}) %collective-permute-start.1) | collective-permute-done | bytes 65568 | tf_op jit(solution)/shard_map/ppermute | solution.py:191
  5.6 0.0 collective-permute-done.refs_1_
  5.6 1.3 %collective-permute-done.2.refs_3_ = bf16[1,8,4096]{2,1,0:T(8,128)(2,1)S(1)} collective-permute-done((bf16[1,8,4096]{2,1,0:T(8,128)(2,1)}, bf16[1,8,4096]{2,1,0:T(8,128)(2,1)S(1)}, u32[]{:S(2)}, u32[]{:S(2)}) %collective-permute-start.2) | collective-permute-done | bytes 65568 | tf_op jit(solution)/shard_map/ppermute | solution.py:191
  7.0 0.0 copy-done.1
  7.0 0.0 copy-done.2
  7.0 0.0 copy-done
  7.0 0.0 copy-start.4
  7.0 1.3 %edges.1 = (bf16[33,32,128]{2,1,0:T(8,128)(2,1)S(1)}, bf16[32,256]{1,0:T(8,128)(2,1)S(1)}, bf16[32,256]{1,0:T(8,128)(2,1)S(1)}) custom-call(s32[5,128]{1,0:T(8,128)S(1)} %get-tuple-element.16.slots, s32[448]{0:T(512)S(1)} %copy-done.2, bf16[1,8,4096]{2,1,0:T(8,128)(2,1)S(1)} %copy-done.1, bf16[1,8,4096]{2,1,0:T(8,128)(2,1)S(1)} %collective-permute-done.refs_1_, ...), custom_call_target="tpu_custom_call" | custom-call | flops 524288 | bytes 1024 | tf_op jit(solution)/shard_map/edges/pallas_call | solution.py:210
  8.3 0.5 %collective-permute-start.3 = (bf16[32,256]{1,0:T(8,128)(2,1)S(1)}, bf16[32,256]{1,0:T(8,128)(2,1)S(1)}, u32[]{:S(2)}, u32[]{:S(2)}) collective-permute-start(bf16[32,256]{1,0:T(8,128)(2,1)S(1)} %get-tuple-element.21), channel_id=1, source_target_pairs={{0,4},{4,0},{8,12},{12,8},{1,5},{5,1},{9,13},{13,9},{2,6},{6,2},{1... | collective-permute-start | bytes 49160 | tf_op jit(solution)/shard_map/ppermute | solution.py:191
  8.9 1.3 %collective-permute-start.4 = (bf16[32,256]{1,0:T(8,128)(2,1)S(1)}, bf16[32,256]{1,0:T(8,128)(2,1)S(1)}, u32[]{:S(2)}, u32[]{:S(2)}) collective-permute-start(bf16[32,256]{1,0:T(8,128)(2,1)S(1)} %get-tuple-element.22), channel_id=1, source_target_pairs={{0,12},{4,8},{8,4},{12,0},{1,13},{5,9},{9,5},{13,1},{2,14},{6,10},... | collective-permute-start | bytes 49160 | tf_op jit(solution)/shard_map/ppermute | solution.py:225
  10.2 0.0 slice-start
  10.2 0.0 slice-start.1
  10.2 3.4 %gate.2.gate_sums = f32[58,32,128]{2,1,0:T(8,128)S(1)} custom-call(s32[5,128]{1,0:T(8,128)S(1)} %get-tuple-element.16.slots, s32[448]{0:T(512)S(1)} %copy-done.2, bf16[33,32,128]{2,1,0:T(8,128)(2,1)S(1)} %get-tuple-element.18.by_col, bf16[448,128,128]{2,1,0:T(8,128)(2,1)S(1)} %copy-done), custom_call_target="tpu_custom_call" | custom-call | flops 1048576 | bytes 1024 | tf_op jit(solution)/shard_map/gate/pallas_call | solution.py:228
  13.6 0.0 copy-done.4
  13.6 0.0 slice-start.2
  13.6 0.0 slice-start.3
  13.6 0.0 copy-start.3
  13.6 3.7 %up.4 = (bf16[58,32,128]{2,1,0:T(8,128)(2,1)S(1)}, f32[2,2,32,128]{3,2,1,0:T(8,128)S(1)}) custom-call(s32[5,128]{1,0:T(8,128)S(1)} %get-tuple-element.16.slots, s32[448]{0:T(512)S(1)} %copy-done.2, bf16[33,32,128]{2,1,0:T(8,128)(2,1)S(1)} %get-tuple-element.18.by_col, bf16[448,128,128]{2,1,0:T(8,128)(2,1)S(1)} %copy-done.4, f32[58,32,128]{2,1,0:T(8,128)S(1)} %gate.2.gate_sums), custom_call_target="tpu_custom_call" | custom-call | flops 8589934592 | bytes 1024 | tf_op jit(solution)/shard_map/up/pallas_call | solution.py:237
  17.3 0.0 collective-permute-done.3.from_inner
  17.3 0.0 collective-permute-done.4.from_outer
  17.3 0.0 slice-done
  17.3 0.0 slice-done.1
  17.3 0.0 slice-done.2
  17.3 0.0 slice-done.3
  17.3 0.0 copy-done.3
  17.4 3.1 %down.2 = (f32[32,1024]{1,0:T(8,128)S(1)}, bf16[32,1024]{1,0:T(8,128)(2,1)S(1)}, bf16[32,1024]{1,0:T(8,128)(2,1)S(1)}, bf16[32,1024]{1,0:T(8,128)(2,1)S(1)}) custom-call(s32[5,128]{1,0:T(8,128)S(1)} %get-tuple-element.16.slots, s32[448]{0:T(512)S(1)} %copy-done.3, bf16[58,32,128]{2,1,0:T(8,128)(2,1)S(1)} %get-tuple-element.19.hidden, ...), custom_call_target="tpu_custom_call" | custom-call | flops 262144 | bytes 1024 | tf_op jit(solution)/shard_map/down/pallas_call | solution.py:250
  20.5 0.9 %collective-permute-start.5 = (bf16[32,1024]{1,0:T(8,128)(2,1)S(1)}, bf16[32,1024]{1,0:T(8,128)(2,1)S(1)}, u32[]{:S(2)}, u32[]{:S(2)}) collective-permute-start(bf16[32,1024]{1,0:T(8,128)(2,1)S(1)} %get-tuple-element.24), channel_id=1, source_target_pairs={{0,8},{4,12},{8,0},{12,4},{1,9},{5,13},{9,1},{13,5},{2,10},{6,14},... | collective-permute-start | bytes 196616 | tf_op jit(solution)/shard_map/ppermute | solution.py:191
  21.4 0.6 %collective-permute-start.6 = (bf16[32,1024]{1,0:T(8,128)(2,1)S(1)}, bf16[32,1024]{1,0:T(8,128)(2,1)S(1)}, u32[]{:S(2)}, u32[]{:S(2)}) collective-permute-start(bf16[32,1024]{1,0:T(8,128)(2,1)S(1)} %get-tuple-element.25), channel_id=1, source_target_pairs={{0,12},{4,8},{8,4},{12,0},{1,13},{5,9},{9,5},{13,1},{2,14},{6,10},... | collective-permute-start | bytes 196616 | tf_op jit(solution)/shard_map/ppermute | solution.py:191
  22.0 0.7 %collective-permute-start.7 = (bf16[32,1024]{1,0:T(8,128)(2,1)S(1)}, bf16[32,1024]{1,0:T(8,128)(2,1)S(1)}, u32[]{:S(2)}, u32[]{:S(2)}) collective-permute-start(bf16[32,1024]{1,0:T(8,128)(2,1)S(1)} %get-tuple-element.26), channel_id=1, source_target_pairs={{0,4},{4,0},{8,12},{12,8},{1,5},{5,1},{9,13},{13,9},{2,6},{6,2},{1... | collective-permute-start | bytes 196616 | tf_op jit(solution)/shard_map/ppermute | solution.py:191
  22.7 2.6 %collective-permute-done.5 = bf16[32,1024]{1,0:T(8,128)(2,1)S(1)} collective-permute-done((bf16[32,1024]{1,0:T(8,128)(2,1)S(1)}, bf16[32,1024]{1,0:T(8,128)(2,1)S(1)}, u32[]{:S(2)}, u32[]{:S(2)}) %collective-permute-start.5) | collective-permute-done | bytes 65568 | tf_op jit(solution)/shard_map/ppermute | solution.py:191
  25.2 0.5 %collective-permute-done.6 = bf16[32,1024]{1,0:T(8,128)(2,1)S(1)} collective-permute-done((bf16[32,1024]{1,0:T(8,128)(2,1)S(1)}, bf16[32,1024]{1,0:T(8,128)(2,1)S(1)}, u32[]{:S(2)}, u32[]{:S(2)}) %collective-permute-start.6) | collective-permute-done | bytes 65568 | tf_op jit(solution)/shard_map/ppermute | solution.py:191
  25.8 0.0 collective-permute-done.7
  25.8 0.7 %fusion = bf16[4,8,1024]{2,1,0:T(8,128)(2,1)} fusion(bf16[32,1024]{1,0:T(8,128)(2,1)S(1)} %collective-permute-done.7, bf16[32,1024]{1,0:T(8,128)(2,1)S(1)} %collective-permute-done.6, f32[32,1024]{1,0:T(8,128)S(1)} %get-tuple-element.23, bf16[32,1024]{1,0:T(8,128)(2,1)S(1)} %collective-permute-done.5), kind=kLoop, calls=%fused_computation.1 | loop fusion | flops 229376 | bytes 393216 | tf_op jit(solution)/shard_map/reshape | solution.py:270
  (1 shorter events, 0.0 us)
Async XLA Ops:
  0.0 7.0 %copy-start.1 = (bf16[1,8,4096]{2,1,0:T(8,128)(2,1)S(1)}, bf16[1,8,4096]{2,1,0:T(8,128)(2,1)}, u32[]{:S(2)}) copy-start(bf16[1,8,4096]{2,1,0:T(8,128)(2,1)} %refs_0_.1) | copy-start | bytes 196612
  0.0 7.0 %copy-start.2 = (s32[448]{0:T(512)S(1)}, s32[448]{0:T(512)}, u32[]{:S(2)}) copy-start(s32[448]{0:T(512)} %cols.6) | copy-start | bytes 5380
  0.0 7.0 %copy-start = (bf16[448,128,128]{2,1,0:T(8,128)(2,1)S(1)}, bf16[448,128,128]{2,1,0:T(8,128)(2,1)}, u32[]{:S(2)}) copy-start(bf16[448,128,128]{2,1,0:T(8,128)(2,1)} %gate.3) | copy-start | bytes 44040196
  0.0 5.6 %collective-permute-start.1 = (bf16[1,8,4096]{2,1,0:T(8,128)(2,1)}, bf16[1,8,4096]{2,1,0:T(8,128)(2,1)S(1)}, u32[]{:S(2)}, u32[]{:S(2)}) collective-permute-start(bf16[1,8,4096]{2,1,0:T(8,128)(2,1)} %refs_0_.1), channel_id=1, source_target_pairs={{0,8},{4,12},{8,0},{12,4},{1,9},{5,13},{9,1},{13,5},{2,10},{6,14},... | collective-permute-start | bytes 196616 | tf_op jit(solution)/shard_map/ppermute | solution.py:191
  3.0 2.6 %collective-permute-start = (bf16[1,8,4096]{2,1,0:T(8,128)(2,1)}, bf16[1,8,4096]{2,1,0:T(8,128)(2,1)S(1)}, u32[]{:S(2)}, u32[]{:S(2)}) collective-permute-start(bf16[1,8,4096]{2,1,0:T(8,128)(2,1)} %refs_0_.1), channel_id=1, source_target_pairs={{0,4},{4,0},{8,12},{12,8},{1,5},{5,1},{9,13},{13,9},{2,6},{6,2},{1... | collective-permute-start | bytes 196616 | tf_op jit(solution)/shard_map/ppermute | solution.py:191
  3.0 4.0 %collective-permute-start.2 = (bf16[1,8,4096]{2,1,0:T(8,128)(2,1)}, bf16[1,8,4096]{2,1,0:T(8,128)(2,1)S(1)}, u32[]{:S(2)}, u32[]{:S(2)}) collective-permute-start(bf16[1,8,4096]{2,1,0:T(8,128)(2,1)} %refs_0_.1), channel_id=1, source_target_pairs={{0,12},{4,8},{8,4},{12,0},{1,13},{5,9},{9,5},{13,1},{2,14},{6,10},... | collective-permute-start | bytes 196616 | tf_op jit(solution)/shard_map/ppermute | solution.py:191
  7.0 6.6 %copy-start.4 = (bf16[448,128,128]{2,1,0:T(8,128)(2,1)S(1)}, bf16[448,128,128]{2,1,0:T(8,128)(2,1)}, u32[]{:S(2)}) copy-start(bf16[448,128,128]{2,1,0:T(8,128)(2,1)} %up.5) | copy-start | bytes 44040196
  8.3 8.9 %collective-permute-start.3 = (bf16[32,256]{1,0:T(8,128)(2,1)S(1)}, bf16[32,256]{1,0:T(8,128)(2,1)S(1)}, u32[]{:S(2)}, u32[]{:S(2)}) collective-permute-start(bf16[32,256]{1,0:T(8,128)(2,1)S(1)} %get-tuple-element.21), channel_id=1, source_target_pairs={{0,4},{4,0},{8,12},{12,8},{1,5},{5,1},{9,13},{13,9},{2,6},{6,2},{1... | collective-permute-start | bytes 49160 | tf_op jit(solution)/shard_map/ppermute | solution.py:191
  8.9 8.4 %collective-permute-start.4 = (bf16[32,256]{1,0:T(8,128)(2,1)S(1)}, bf16[32,256]{1,0:T(8,128)(2,1)S(1)}, u32[]{:S(2)}, u32[]{:S(2)}) collective-permute-start(bf16[32,256]{1,0:T(8,128)(2,1)S(1)} %get-tuple-element.22), channel_id=1, source_target_pairs={{0,12},{4,8},{8,4},{12,0},{1,13},{5,9},{9,5},{13,1},{2,14},{6,10},... | collective-permute-start | bytes 49160 | tf_op jit(solution)/shard_map/ppermute | solution.py:225
  10.2 7.1 %slice-start = ((s8[14680064]{0:T(1024)(128)(4,1)}), s8[2097152]{0:T(1024)(128)(4,1)S(1)}, s32[]{:S(2)}) async-start(s8[14680064]{0:T(1024)(128)(4,1)} %bitcast.2), calls=%async_computation | async-start | bytes 4194304
  10.2 7.1 %slice-start.1 = ((s8[14680064]{0:T(1024)(128)(4,1)}), s8[4194304]{0:T(1024)(128)(4,1)S(1)}, s32[]{:S(2)}) async-start(s8[14680064]{0:T(1024)(128)(4,1)} %bitcast.2), calls=%async_computation.1 | async-start | bytes 8388608
  13.6 3.8 %slice-start.2 = ((s8[14680064]{0:T(1024)(128)(4,1)}), s8[4194304]{0:T(1024)(128)(4,1)S(1)}, s32[]{:S(2)}) async-start(s8[14680064]{0:T(1024)(128)(4,1)} %bitcast.2), calls=%async_computation.2 | async-start | bytes 8388608
  13.6 3.8 %slice-start.3 = ((s8[14680064]{0:T(1024)(128)(4,1)}), s8[4194304]{0:T(1024)(128)(4,1)S(1)}, s32[]{:S(2)}) async-start(s8[14680064]{0:T(1024)(128)(4,1)} %bitcast.2), calls=%async_computation.3 | async-start | bytes 8388608
  13.6 3.8 %copy-start.3 = (s32[448]{0:T(512)S(1)}, s32[448]{0:T(512)}, u32[]{:S(2)}) copy-start(s32[448]{0:T(512)} %cols.7) | copy-start | bytes 5380
  20.5 4.8 %collective-permute-start.5 = (bf16[32,1024]{1,0:T(8,128)(2,1)S(1)}, bf16[32,1024]{1,0:T(8,128)(2,1)S(1)}, u32[]{:S(2)}, u32[]{:S(2)}) collective-permute-start(bf16[32,1024]{1,0:T(8,128)(2,1)S(1)} %get-tuple-element.24), channel_id=1, source_target_pairs={{0,8},{4,12},{8,0},{12,4},{1,9},{5,13},{9,1},{13,5},{2,10},{6,14},... | collective-permute-start | bytes 196616 | tf_op jit(solution)/shard_map/ppermute | solution.py:191
  21.4 4.4 %collective-permute-start.6 = (bf16[32,1024]{1,0:T(8,128)(2,1)S(1)}, bf16[32,1024]{1,0:T(8,128)(2,1)S(1)}, u32[]{:S(2)}, u32[]{:S(2)}) collective-permute-start(bf16[32,1024]{1,0:T(8,128)(2,1)S(1)} %get-tuple-element.25), channel_id=1, source_target_pairs={{0,12},{4,8},{8,4},{12,0},{1,13},{5,9},{9,5},{13,1},{2,14},{6,10},... | collective-permute-start | bytes 196616 | tf_op jit(solution)/shard_map/ppermute | solution.py:191
  22.0 3.8 %collective-permute-start.7 = (bf16[32,1024]{1,0:T(8,128)(2,1)S(1)}, bf16[32,1024]{1,0:T(8,128)(2,1)S(1)}, u32[]{:S(2)}, u32[]{:S(2)}) collective-permute-start(bf16[32,1024]{1,0:T(8,128)(2,1)S(1)} %get-tuple-element.26), channel_id=1, source_target_pairs={{0,4},{4,0},{8,12},{12,8},{1,5},{5,1},{9,13},{13,9},{2,6},{6,2},{1... | collective-permute-start | bytes 196616 | tf_op jit(solution)/shard_map/ppermute | solution.py:191

commit v4 on v3

--- a/solution.py
+++ b/solution.py
@@ -67,10 +67,55 @@
     return slots[lax.shift_right_logical(block, 7), lax.bitwise_and(block, 127)]
 
 
-def edge_kernel(slots, cols, *refs):
-    pieces, (gate, edge_up, by_col, to_inner, to_outer, whole) = refs[:-6], refs[-6:]
-    size = len(pieces)
-    count = cols.shape[0]
+def left_operand(slots, cols, by_col, first):
+    none = by_col.shape[0] - 1
+    even, odd = [], []
+    for q in range(GROUP):
+        col, is_odd = cols[first + q], (slot_of(slots, first + q) & 1) == 1
+        even.append(by_col[jnp.where(is_odd, none, col)])
+        odd.append(by_col[jnp.where(is_odd, col, none)])
+    return jnp.concatenate([jnp.concatenate(even, axis=1), jnp.concatenate(odd, axis=1)], axis=0)
+
+
+def slots_met(slots, first):
+    slot = slot_of(slots, first)
+    return slot + (slot & 1), slot | 1
+
+
+def silu_gate(gate, up):
+    return (gate * (0.5 * jnp.tanh(0.5 * gate) + 0.5) * up).astype(BF16)
+
+
+def edge_groups(count):
+    return [(side, k, first + k * GROUP) for side, first in ((0, 0), (1, count - EDGE)) for k in range(EDGE // GROUP)]
+
+
+def group_sums(slots, cols, by_col, weights, first):
+    left = left_operand(slots, cols, by_col, first)
+    right = weights.reshape(GROUP * 128, 128)
+    return jnp.dot(left, right, preferred_element_type=F32)
+
+
+def add_group(slots, first, part, sums):
+    rows = part.shape[0] // 2
+    at_even, at_odd = slots_met(slots, first)
+    old_even, old_odd = sums[at_even], sums[at_odd]
+    sums[at_even] = old_even + part[:rows]
+    sums[at_odd] = old_odd + part[rows:]
+
+
+def add_rows(slots, cols, by_col, weights, sums, groups, unroll):
+    def step(it, carry):
+        for j in range(unroll):
+            first = (groups[0] + it * unroll + j) * GROUP
+            add_group(slots, first, group_sums(slots, cols, by_col, weights[pl.ds(first, GROUP)], first), sums)
+        return carry
+
+    lax.fori_loop(0, (groups[1] - groups[0]) // unroll, step, 0)
+
+
+def gate_kernel(slots, cols, gate, *refs, unroll):
+    pieces, (by_col, sums, whole) = refs[:-3], refs[-3:]
     col_blocks, rows = by_col.shape[0] - 1, by_col.shape[1]
     me = lax.axis_index("weight")
     for distance, piece in enumerate(pieces):
@@ -79,62 +124,40 @@
     for c in range(col_blocks):
         by_col[c] = merged[:, c * 128 : (c + 1) * 128]
     by_col[col_blocks] = jnp.zeros((rows, 128), BF16)
+    sums[...] = jnp.zeros_like(sums)
+    add_rows(slots, cols, by_col, gate, sums, (0, cols.shape[0] // GROUP), unroll)
+
+
+def edge_kernel(slots, cols, by_col, edge_up, gate_sums, edge_sums, to_inner, to_outer):
+    rows = by_col.shape[1]
+    count = cols.shape[0]
+    totals = [jnp.zeros((rows, 128), F32)] * 2
+    shared = (0, slot_of(slots, count - 1))
+    for side, k, first in edge_groups(count):
+        weights = edge_up[side, k * GROUP : (k + 1) * GROUP]
+        part = group_sums(slots, cols, by_col, weights, first)
+        edge_sums[side, k] = part
+        at_even, at_odd = slots_met(slots, first)
+        totals[side] += jnp.where(at_even == shared[side], part[:rows], 0.0)
+        totals[side] += jnp.where(at_odd == shared[side], part[rows:], 0.0)
     last_flag = slots.shape[0] - 1
-    is_odd = (me & 1) == 1
     parts = []
-    for side, first in ((0, 0), (1, count - EDGE)):
-        mine = slot_of(slots, 0 if side == 0 else count - 1)
-        picked = []
-        for q in range(EDGE):
-            block = first + q
-            picked.append(by_col[jnp.where(slot_of(slots, block) == mine, cols[block], col_blocks)])
-        weights = jnp.concatenate(
-            [gate[first : first + EDGE].reshape(EDGE * 128, 128), edge_up[side].reshape(EDGE * 128, 128)], axis=1
-        )
-        total = jnp.dot(jnp.concatenate(picked, axis=1), weights, preferred_element_type=F32)
-        parts.append(jnp.where(slots[last_flag, side] == 1, total, 0.0).astype(BF16))
+    for side in (0, 1):
+        both = jnp.concatenate([gate_sums[shared[side]], totals[side]], axis=1)
+        parts.append(jnp.where(slots[last_flag, side] == 1, both, 0.0).astype(BF16))
+    is_odd = (lax.axis_index("weight") & 1) == 1
     to_inner[...] = jnp.where(is_odd, parts[0], parts[1])
     to_outer[...] = jnp.where(is_odd, parts[1], parts[0])
 
 
-def silu_gate(gate, up):
-    return (gate / (1 + jnp.exp(-gate)) * up).astype(BF16)
-
-
-def add_rows(slots, cols, by_col, weights, sums, unroll):
-    col_blocks, rows = by_col.shape[0] - 1, by_col.shape[1]
+def up_kernel(slots, cols, by_col, up, edge_sums, gate_sums, hidden, edges, sums, *, unroll):
     count = cols.shape[0]
     sums[...] = jnp.zeros_like(sums)
-
-    def step(it, carry):
-        for j in range(unroll):
-            first = (it * unroll + j) * GROUP
-            slot = slot_of(slots, first)
-            even, odd = [], []
-            for q in range(GROUP):
-                col, is_odd = cols[first + q], (slot_of(slots, first + q) & 1) == 1
-                even.append(by_col[jnp.where(is_odd, col_blocks, col)])
-                odd.append(by_col[jnp.where(is_odd, col, col_blocks)])
-            left = jnp.concatenate([jnp.concatenate(even, axis=1), jnp.concatenate(odd, axis=1)], axis=0)
-            right = weights[pl.ds(first, GROUP)].reshape(GROUP * 128, 128)
-            part = jnp.dot(left, right, preferred_element_type=F32)
-            at_even, at_odd = slot + (slot & 1), slot | 1
-            old_even, old_odd = sums[at_even], sums[at_odd]
-            sums[at_even] = old_even + part[:rows]
-            sums[at_odd] = old_odd + part[rows:]
-        return carry
-
-    lax.fori_loop(0, count // GROUP // unroll, step, 0)
-
-
-def gate_kernel(slots, cols, by_col, gate, sums, *, unroll):
-    add_rows(slots, cols, by_col, gate, sums, unroll)
-
-
-def up_kernel(slots, cols, by_col, up, gate_sums, hidden, edges, sums, *, unroll):
-    add_rows(slots, cols, by_col, up, sums, unroll)
+    for side, k, first in edge_groups(count):
+        add_group(slots, first, edge_sums[side, k], sums)
+    add_rows(slots, cols, by_col, up, sums, (EDGE // GROUP, (count - EDGE) // GROUP), unroll)
     hidden[...] = silu_gate(gate_sums[...], sums[...])
-    for side, slot in enumerate((0, slot_of(slots, cols.shape[0] - 1))):
+    for side, slot in enumerate((0, slot_of(slots, count - 1))):
         edges[side, 0] = gate_sums[slot]
         edges[side, 1] = sums[slot]
 
@@ -204,49 +227,52 @@
         out_specs=(VM, VM),
         scratch_shapes=[pltpu.SMEM(row_starts.shape, jnp.int32), pltpu.SemaphoreType.DMA((3,))],
         compiler_params=limit(4),
-        cost_estimate=cost(2**36),
+        cost_estimate=cost(2**33),
         name="prepare",
     )(in_hbm(row_starts), in_hbm(up_blocks))
-    by_col, to_inner, to_outer = pl.pallas_call(
+    unroll = largest_divisor(count // GROUP, 28)
+    by_col, gate_sums = pl.pallas_call(
+        functools.partial(gate_kernel, unroll=unroll),
+        out_shape=(
+            pltpu.VMEM((col_blocks + 1, rows, width), BF16),
+            pltpu.VMEM((row_slots, rows, width), F32),
+        ),
+        in_specs=[SM, SM] + [VM] * (size + 1),
+        out_specs=(VM, VM),
+        scratch_shapes=[pltpu.VMEM((size, slab, model_width), BF16)],
+        compiler_params=limit(8),
+        cost_estimate=cost(2**20),
+        name="gate",
+    )(slots, gate_cols, in_vmem(gate_blocks), *pieces)
+    edge_sums, to_inner, to_outer = pl.pallas_call(
         edge_kernel,
         out_shape=(
-            pltpu.VMEM((col_blocks + 1, rows, width), BF16),
+            pltpu.VMEM((2, EDGE // GROUP, 2 * rows, width), F32),
             jax.ShapeDtypeStruct((rows, 2 * width), BF16),
             jax.ShapeDtypeStruct((rows, 2 * width), BF16),
         ),
-        in_specs=[SM, SM] + [VM] * (size + 2),
+        in_specs=[SM, SM, VM, VM, VM],
         out_specs=(VM, VM, VM),
-        scratch_shapes=[pltpu.VMEM((size, slab, model_width), BF16)],
         compiler_params=limit(4),
-        cost_estimate=cost(2**19),
+        cost_estimate=cost(2**20),
         name="edges",
-    )(slots, gate_cols, *pieces, in_vmem(gate_blocks), edge_up)
+    )(slots, gate_cols, in_vmem(by_col), edge_up, in_vmem(gate_sums))
     outer_pairs = [(d, (d + 1 if d % 2 else d - 1) % size) for d in range(size)]
     from_outer = lax.ppermute(to_outer, "weight", outer_pairs)
     from_inner = swap(to_inner, 1)
-    unroll = largest_divisor(count // GROUP, 28)
-    gate_sums = pl.pallas_call(
-        functools.partial(gate_kernel, unroll=unroll),
-        out_shape=pltpu.VMEM((row_slots, rows, width), F32),
-        in_specs=[SM, SM, VM, VM],
-        out_specs=VM,
-        compiler_params=limit(8),
-        cost_estimate=cost(2**20),
-        name="gate",
-    )(slots, gate_cols, by_col, in_vmem(gate_blocks))
     hidden, edges = pl.pallas_call(
-        functools.partial(up_kernel, unroll=unroll),
+        functools.partial(up_kernel, unroll=largest_divisor((count - 2 * EDGE) // GROUP, 28)),
         out_shape=(
             pltpu.VMEM((row_slots, rows, width), BF16),
             pltpu.VMEM((2, 2, rows, width), F32),
         ),
-        in_specs=[SM, SM, VM, VM, VM],
+        in_specs=[SM, SM, VM, VM, VM, VM],
         out_specs=(VM, VM),
         scratch_shapes=[pltpu.VMEM((row_slots, rows, width), F32)],
         compiler_params=limit(8),
-        cost_estimate=cost(2**33),
+        cost_estimate=cost(2**20),
         name="up",
-    )(slots, gate_cols, by_col, in_vmem(up_blocks), in_vmem(gate_sums))
+    )(slots, gate_cols, in_vmem(by_col), in_vmem(up_blocks), in_vmem(edge_sums), in_vmem(gate_sums))
     outs = pl.pallas_call(
         functools.partial(down_kernel, unroll=unroll),
         out_shape=tuple(
@@ -260,9 +286,9 @@
             pltpu.VMEM((2, col_blocks, rows, width), F32),
         ],
         compiler_params=limit(8),
-        cost_estimate=cost(2**18),
+        cost_estimate=cost(2**20),
         name="down",
-    )(slots, down_cols, hidden, edges, from_inner, from_outer, in_vmem(down_blocks))
+    )(slots, down_cols, in_vmem(hidden), in_vmem(edges), from_inner, from_outer, in_vmem(down_blocks))
     received = {distance: swap(outs[distance], distance) for distance in order}
     total = outs[0]
     for distance in order:

time: 26.6 us -> 25.8 us (0.970)
  waiting for transfers between devices: 4.7 us -> 4.27 us
  Pallas kernels: 13.6 us -> 13.2 us
    pallas_call x3, Pallas kernels: 8.38 us -> 7.87 us  [the longest x1 3.49 us: per_device(): pl.pallas_call(functools.partial(gate_kernel, unroll=unroll), out_shape=(...]
    ppermute x7, waiting for transfers between devices: 4.7 us -> 4.27 us  [swap(): lax.ppermute(value, 'weight', [(d, d ^ distance) for d in range(size)])]
  transfers between devices with their start and end apart: 8 -> 8, of which waited for: 4 -> 3; matrix products, arithmetic and copies ran while one was open for 0% -> 0% of each run, Pallas kernels for 35% -> 21%
where the time goes in v4:
time: 25.8 us; the launch traced here: 25.6 us
  Pallas kernels  13.2 us (51%)
  starting transfers between devices  7.23 us (28%)
  waiting for transfers between devices  4.27 us (17%)
  other arithmetic  0.66 us (3%)
    ppermute x7, starting transfers between devices, swap(): lax.ppermute(value, 'weight', [(d, d ^ distance) for d in range(size)])  5.96 us
    ppermute x7, waiting for transfers between devices, swap(): lax.ppermute(value, 'weight', [(d, d ^ distance) for d in range(size)])  4.27 us
    pallas_call x1, Pallas kernels, per_device(): pl.pallas_call(functools.partial(gate_kernel, unroll=unroll), out_shape=(...  3.49 us
    pallas_call x1, Pallas kernels, per_device(): pl.pallas_call(functools.partial(up_kernel, unroll=largest_divisor((count...  3.32 us
    pallas_call x1, Pallas kernels, per_device(): pl.pallas_call(functools.partial(down_kernel, unroll=unroll), out_shape=t...  3.1 us
    pallas_call x1, Pallas kernels, per_device(): pl.pallas_call(functools.partial(prepare_kernel, count=count), out_shape=...  2.18 us
    ppermute x1, starting transfers between devices, per_device(): from_outer = lax.ppermute(to_outer, 'weight', outer_pairs)  1.27 us
    pallas_call x1, Pallas kernels, per_device(): pl.pallas_call(edge_kernel, out_shape=(pltpu.VMEM((2, EDGE // GROUP, 2 *...  1.06 us
  transfers between devices with their start and end apart: 8, of which 3 were waited for; matrix products, arithmetic and copies ran while one was open for 0% of the time, Pallas kernels for 21%

profile of v4, /device:TPU:0, one launch (start us, length us, event | category | flops | bytes accessed | tf_op | source)
XLA Modules:
  0.0 25.6 jit_solution(15726256693625426073)
XLA Ops:
  0.0 0.0 copy-start.1
  0.0 0.0 copy-start.2
  0.0 0.0 copy-start
  0.0 3.0 %collective-permute-start.1 = (bf16[1,8,4096]{2,1,0:T(8,128)(2,1)}, bf16[1,8,4096]{2,1,0:T(8,128)(2,1)S(1)}, u32[]{:S(2)}, u32[]{:S(2)}) collective-permute-start(bf16[1,8,4096]{2,1,0:T(8,128)(2,1)} %refs_0_.1), channel_id=1, source_target_pairs={{0,8},{4,12},{8,0},{12,4},{1,9},{5,13},{9,1},{13,5},{2,10},{6,14},... | collective-permute-start | bytes 196616 | tf_op jit(solution)/shard_map/ppermute | solution.py:214
  3.0 0.0 collective-permute-start
  3.0 0.2 collective-permute-start.2
  3.2 0.0 slice-start
  3.2 0.0 slice-start.1
  3.2 0.0 slice-start.2
  3.2 2.2 %prepare.1 = (s32[5,128]{1,0:T(8,128)S(1)}, bf16[2,24,128,128]{3,2,1,0:T(8,128)(2,1)S(1)}) custom-call(s32[113]{0:T(128)} %starts.1, bf16[448,128,128]{2,1,0:T(8,128)(2,1)} %up.5), custom_call_target="tpu_custom_call" | custom-call | flops 8589934592 | bytes 1024 | tf_op jit(solution)/shard_map/prepare/pallas_call | solution.py:220
  5.4 0.2 collective-permute-done.1.refs_2_
  5.6 0.0 collective-permute-done.refs_1_
  5.6 1.3 %collective-permute-done.2.refs_3_ = bf16[1,8,4096]{2,1,0:T(8,128)(2,1)S(1)} collective-permute-done((bf16[1,8,4096]{2,1,0:T(8,128)(2,1)}, bf16[1,8,4096]{2,1,0:T(8,128)(2,1)S(1)}, u32[]{:S(2)}, u32[]{:S(2)}) %collective-permute-start.2) | collective-permute-done | bytes 65568 | tf_op jit(solution)/shard_map/ppermute | solution.py:214
  7.0 0.0 copy-done.1
  7.0 0.0 copy-done.2
  7.0 0.0 copy-done
  7.0 0.0 slice-start.3
  7.0 0.0 slice-start.4
  7.0 0.0 slice-start.5
  7.0 0.0 copy-start.3
  7.0 3.5 %gate.2 = (bf16[33,32,128]{2,1,0:T(8,128)(2,1)S(1)}, f32[58,32,128]{2,1,0:T(8,128)S(1)}) custom-call(s32[5,128]{1,0:T(8,128)S(1)} %get-tuple-element.18.slots, s32[448]{0:T(512)S(1)} %copy-done.2, bf16[448,128,128]{2,1,0:T(8,128)(2,1)S(1)} %copy-done, bf16[1,8,4096]{2,1,0:T(8,128)(2,1)S(1)} %copy-done.1, ...), custom_call_target="tpu_custom_call" | custom-call | flops 1048576 | bytes 1024 | tf_op jit(solution)/shard_map/gate/pallas_call | solution.py:234
  10.5 0.0 slice-start.6
  10.5 1.1 %edges.1 = (f32[2,3,64,128]{3,2,1,0:T(8,128)S(1)}, bf16[32,256]{1,0:T(8,128)(2,1)S(1)}, bf16[32,256]{1,0:T(8,128)(2,1)S(1)}) custom-call(s32[5,128]{1,0:T(8,128)S(1)} %get-tuple-element.18.slots, s32[448]{0:T(512)S(1)} %copy-done.2, bf16[33,32,128]{2,1,0:T(8,128)(2,1)S(1)} %get-tuple-element.19.by_col, ...), custom_call_target="tpu_custom_call" | custom-call | flops 1048576 | bytes 1024 | tf_op jit(solution)/shard_map/edges/pallas_call | solution.py:247
  11.6 0.5 %collective-permute-start.3 = (bf16[32,256]{1,0:T(8,128)(2,1)S(1)}, bf16[32,256]{1,0:T(8,128)(2,1)S(1)}, u32[]{:S(2)}, u32[]{:S(2)}) collective-permute-start(bf16[32,256]{1,0:T(8,128)(2,1)S(1)} %get-tuple-element.25), channel_id=1, source_target_pairs={{0,4},{4,0},{8,12},{12,8},{1,5},{5,1},{9,13},{13,9},{2,6},{6,2},{1... | collective-permute-start | bytes 49160 | tf_op jit(solution)/shard_map/ppermute | solution.py:214
  12.2 1.3 %collective-permute-start.4 = (bf16[32,256]{1,0:T(8,128)(2,1)S(1)}, bf16[32,256]{1,0:T(8,128)(2,1)S(1)}, u32[]{:S(2)}, u32[]{:S(2)}) collective-permute-start(bf16[32,256]{1,0:T(8,128)(2,1)S(1)} %get-tuple-element.26), channel_id=1, source_target_pairs={{0,12},{4,8},{8,4},{12,0},{1,13},{5,9},{9,5},{13,1},{2,14},{6,10},... | collective-permute-start | bytes 49160 | tf_op jit(solution)/shard_map/ppermute | solution.py:261
  13.4 0.0 slice-done
  13.4 0.0 slice-done.1
  13.4 0.0 slice-done.2
  13.4 0.0 slice-done.3
  13.4 0.0 slice-start.7
  13.5 3.3 %up.4 = (bf16[58,32,128]{2,1,0:T(8,128)(2,1)S(1)}, f32[2,2,32,128]{3,2,1,0:T(8,128)S(1)}) custom-call(s32[5,128]{1,0:T(8,128)S(1)} %get-tuple-element.18.slots, s32[448]{0:T(512)S(1)} %copy-done.2, bf16[33,32,128]{2,1,0:T(8,128)(2,1)S(1)} %get-tuple-element.19.by_col, bf16[448,128,128]{2,1,0:T(8,128)(2,1)S(1)} %bitcast.3, ...), custom_call_target="tpu_custom_call" | custom-call | flops 1048576 | bytes 1024 | tf_op jit(solution)/shard_map/up/pallas_call | solution.py:263
  16.8 0.0 collective-permute-done.3.from_inner
  16.8 0.0 collective-permute-done.4.from_outer
  16.8 0.0 slice-done.4
  16.8 0.0 slice-done.5
  16.8 0.0 copy-done.3
  16.8 0.0 slice-done.6
  16.9 0.0 slice-done.7
  16.9 3.1 %down.2 = (f32[32,1024]{1,0:T(8,128)S(1)}, bf16[32,1024]{1,0:T(8,128)(2,1)S(1)}, bf16[32,1024]{1,0:T(8,128)(2,1)S(1)}, bf16[32,1024]{1,0:T(8,128)(2,1)S(1)}) custom-call(s32[5,128]{1,0:T(8,128)S(1)} %get-tuple-element.18.slots, s32[448]{0:T(512)S(1)} %copy-done.3, bf16[58,32,128]{2,1,0:T(8,128)(2,1)S(1)} %get-tuple-element.23.hidden, ...), custom_call_target="tpu_custom_call" | custom-call | flops 1048576 | bytes 1024 | tf_op jit(solution)/shard_map/down/pallas_call | solution.py:276
  20.0 0.5 %collective-permute-start.5 = (bf16[32,1024]{1,0:T(8,128)(2,1)S(1)}, bf16[32,1024]{1,0:T(8,128)(2,1)S(1)}, u32[]{:S(2)}, u32[]{:S(2)}) collective-permute-start(bf16[32,1024]{1,0:T(8,128)(2,1)S(1)} %get-tuple-element.28), channel_id=1, source_target_pairs={{0,8},{4,12},{8,0},{12,4},{1,9},{5,13},{9,1},{13,5},{2,10},{6,14},... | collective-permute-start | bytes 196616 | tf_op jit(solution)/shard_map/ppermute | solution.py:214
  20.5 1.0 %collective-permute-start.6 = (bf16[32,1024]{1,0:T(8,128)(2,1)S(1)}, bf16[32,1024]{1,0:T(8,128)(2,1)S(1)}, u32[]{:S(2)}, u32[]{:S(2)}) collective-permute-start(bf16[32,1024]{1,0:T(8,128)(2,1)S(1)} %get-tuple-element.29), channel_id=1, source_target_pairs={{0,12},{4,8},{8,4},{12,0},{1,13},{5,9},{9,5},{13,1},{2,14},{6,10},... | collective-permute-start | bytes 196616 | tf_op jit(solution)/shard_map/ppermute | solution.py:214
  21.5 0.7 %collective-permute-start.7 = (bf16[32,1024]{1,0:T(8,128)(2,1)S(1)}, bf16[32,1024]{1,0:T(8,128)(2,1)S(1)}, u32[]{:S(2)}, u32[]{:S(2)}) collective-permute-start(bf16[32,1024]{1,0:T(8,128)(2,1)S(1)} %get-tuple-element.30), channel_id=1, source_target_pairs={{0,4},{4,0},{8,12},{12,8},{1,5},{5,1},{9,13},{13,9},{2,6},{6,2},{1... | collective-permute-start | bytes 196616 | tf_op jit(solution)/shard_map/ppermute | solution.py:214
  22.2 2.7 %collective-permute-done.5 = bf16[32,1024]{1,0:T(8,128)(2,1)S(1)} collective-permute-done((bf16[32,1024]{1,0:T(8,128)(2,1)S(1)}, bf16[32,1024]{1,0:T(8,128)(2,1)S(1)}, u32[]{:S(2)}, u32[]{:S(2)}) %collective-permute-start.5) | collective-permute-done | bytes 65568 | tf_op jit(solution)/shard_map/ppermute | solution.py:214
  24.9 0.0 collective-permute-done.6
  24.9 0.0 collective-permute-done.7
  24.9 0.7 %fusion = bf16[4,8,1024]{2,1,0:T(8,128)(2,1)} fusion(bf16[32,1024]{1,0:T(8,128)(2,1)S(1)} %collective-permute-done.7, bf16[32,1024]{1,0:T(8,128)(2,1)S(1)} %collective-permute-done.6, f32[32,1024]{1,0:T(8,128)S(1)} %get-tuple-element.27, bf16[32,1024]{1,0:T(8,128)(2,1)S(1)} %collective-permute-done.5), kind=kLoop, calls=%fused_computation.1 | loop fusion | flops 229376 | bytes 393216 | tf_op jit(solution)/shard_map/reshape | solution.py:296
  (2 shorter events, 0.0 us)
Async XLA Ops:
  0.0 7.0 %copy-start.1 = (bf16[1,8,4096]{2,1,0:T(8,128)(2,1)S(1)}, bf16[1,8,4096]{2,1,0:T(8,128)(2,1)}, u32[]{:S(2)}) copy-start(bf16[1,8,4096]{2,1,0:T(8,128)(2,1)} %refs_0_.1) | copy-start | bytes 196612
  0.0 7.0 %copy-start.2 = (s32[448]{0:T(512)S(1)}, s32[448]{0:T(512)}, u32[]{:S(2)}) copy-start(s32[448]{0:T(512)} %cols.6) | copy-start | bytes 5380
  0.0 7.0 %copy-start = (bf16[448,128,128]{2,1,0:T(8,128)(2,1)S(1)}, bf16[448,128,128]{2,1,0:T(8,128)(2,1)}, u32[]{:S(2)}) copy-start(bf16[448,128,128]{2,1,0:T(8,128)(2,1)} %gate.3) | copy-start | bytes 44040196
  0.0 5.6 %collective-permute-start.1 = (bf16[1,8,4096]{2,1,0:T(8,128)(2,1)}, bf16[1,8,4096]{2,1,0:T(8,128)(2,1)S(1)}, u32[]{:S(2)}, u32[]{:S(2)}) collective-permute-start(bf16[1,8,4096]{2,1,0:T(8,128)(2,1)} %refs_0_.1), channel_id=1, source_target_pairs={{0,8},{4,12},{8,0},{12,4},{1,9},{5,13},{9,1},{13,5},{2,10},{6,14},... | collective-permute-start | bytes 196616 | tf_op jit(solution)/shard_map/ppermute | solution.py:214
  3.0 2.6 %collective-permute-start = (bf16[1,8,4096]{2,1,0:T(8,128)(2,1)}, bf16[1,8,4096]{2,1,0:T(8,128)(2,1)S(1)}, u32[]{:S(2)}, u32[]{:S(2)}) collective-permute-start(bf16[1,8,4096]{2,1,0:T(8,128)(2,1)} %refs_0_.1), channel_id=1, source_target_pairs={{0,4},{4,0},{8,12},{12,8},{1,5},{5,1},{9,13},{13,9},{2,6},{6,2},{1... | collective-permute-start | bytes 196616 | tf_op jit(solution)/shard_map/ppermute | solution.py:214
  3.0 4.0 %collective-permute-start.2 = (bf16[1,8,4096]{2,1,0:T(8,128)(2,1)}, bf16[1,8,4096]{2,1,0:T(8,128)(2,1)S(1)}, u32[]{:S(2)}, u32[]{:S(2)}) collective-permute-start(bf16[1,8,4096]{2,1,0:T(8,128)(2,1)} %refs_0_.1), channel_id=1, source_target_pairs={{0,12},{4,8},{8,4},{12,0},{1,13},{5,9},{9,5},{13,1},{2,14},{6,10},... | collective-permute-start | bytes 196616 | tf_op jit(solution)/shard_map/ppermute | solution.py:214
  3.2 10.2 %slice-start = ((s8[14680064]{0:T(1024)(128)(4,1)}), s8[4194304]{0:T(1024)(128)(4,1)S(1)}, s32[]{:S(2)}) async-start(s8[14680064]{0:T(1024)(128)(4,1)} %bitcast.2), calls=%async_computation | async-start | bytes 8388608
  3.2 10.2 %slice-start.1 = ((s8[14680064]{0:T(1024)(128)(4,1)}), s8[4194304]{0:T(1024)(128)(4,1)S(1)}, s32[]{:S(2)}) async-start(s8[14680064]{0:T(1024)(128)(4,1)} %bitcast.2), calls=%async_computation.1 | async-start | bytes 8388608
  3.2 10.2 %slice-start.2 = ((s8[14680064]{0:T(1024)(128)(4,1)}), s8[4194304]{0:T(1024)(128)(4,1)S(1)}, s32[]{:S(2)}) async-start(s8[14680064]{0:T(1024)(128)(4,1)} %bitcast.2), calls=%async_computation.2 | async-start | bytes 8388608
  7.0 6.5 %slice-start.3 = ((s8[14680064]{0:T(1024)(128)(4,1)}), s8[2097152]{0:T(1024)(128)(4,1)S(1)}, s32[]{:S(2)}) async-start(s8[14680064]{0:T(1024)(128)(4,1)} %bitcast.2), calls=%async_computation.3 | async-start | bytes 4194304
  7.0 9.8 %slice-start.4 = ((s8[14680064]{0:T(1024)(128)(4,1)}), s8[4194304]{0:T(1024)(128)(4,1)S(1)}, s32[]{:S(2)}) async-start(s8[14680064]{0:T(1024)(128)(4,1)} %bitcast.4), calls=%async_computation.4 | async-start | bytes 8388608
  7.0 9.8 %slice-start.5 = ((s8[14680064]{0:T(1024)(128)(4,1)}), s8[4194304]{0:T(1024)(128)(4,1)S(1)}, s32[]{:S(2)}) async-start(s8[14680064]{0:T(1024)(128)(4,1)} %bitcast.4), calls=%async_computation.5 | async-start | bytes 8388608
  7.0 9.8 %copy-start.3 = (s32[448]{0:T(512)S(1)}, s32[448]{0:T(512)}, u32[]{:S(2)}) copy-start(s32[448]{0:T(512)} %cols.7) | copy-start | bytes 5380
  10.5 6.3 %slice-start.6 = ((s8[14680064]{0:T(1024)(128)(4,1)}), s8[4194304]{0:T(1024)(128)(4,1)S(1)}, s32[]{:S(2)}) async-start(s8[14680064]{0:T(1024)(128)(4,1)} %bitcast.4), calls=%async_computation.6 | async-start | bytes 8388608
  11.6 5.2 %collective-permute-start.3 = (bf16[32,256]{1,0:T(8,128)(2,1)S(1)}, bf16[32,256]{1,0:T(8,128)(2,1)S(1)}, u32[]{:S(2)}, u32[]{:S(2)}) collective-permute-start(bf16[32,256]{1,0:T(8,128)(2,1)S(1)} %get-tuple-element.25), channel_id=1, source_target_pairs={{0,4},{4,0},{8,12},{12,8},{1,5},{5,1},{9,13},{13,9},{2,6},{6,2},{1... | collective-permute-start | bytes 49160 | tf_op jit(solution)/shard_map/ppermute | solution.py:214
  12.2 4.6 %collective-permute-start.4 = (bf16[32,256]{1,0:T(8,128)(2,1)S(1)}, bf16[32,256]{1,0:T(8,128)(2,1)S(1)}, u32[]{:S(2)}, u32[]{:S(2)}) collective-permute-start(bf16[32,256]{1,0:T(8,128)(2,1)S(1)} %get-tuple-element.26), channel_id=1, source_target_pairs={{0,12},{4,8},{8,4},{12,0},{1,13},{5,9},{9,5},{13,1},{2,14},{6,10},... | collective-permute-start | bytes 49160 | tf_op jit(solution)/shard_map/ppermute | solution.py:261
  13.4 3.4 %slice-start.7 = ((s8[14680064]{0:T(1024)(128)(4,1)}), s8[2097152]{0:T(1024)(128)(4,1)S(1)}, s32[]{:S(2)}) async-start(s8[14680064]{0:T(1024)(128)(4,1)} %bitcast.4), calls=%async_computation.7 | async-start | bytes 4194304
  20.0 4.9 %collective-permute-start.5 = (bf16[32,1024]{1,0:T(8,128)(2,1)S(1)}, bf16[32,1024]{1,0:T(8,128)(2,1)S(1)}, u32[]{:S(2)}, u32[]{:S(2)}) collective-permute-start(bf16[32,1024]{1,0:T(8,128)(2,1)S(1)} %get-tuple-element.28), channel_id=1, source_target_pairs={{0,8},{4,12},{8,0},{12,4},{1,9},{5,13},{9,1},{13,5},{2,10},{6,14},... | collective-permute-start | bytes 196616 | tf_op jit(solution)/shard_map/ppermute | solution.py:214
  20.5 4.4 %collective-permute-start.6 = (bf16[32,1024]{1,0:T(8,128)(2,1)S(1)}, bf16[32,1024]{1,0:T(8,128)(2,1)S(1)}, u32[]{:S(2)}, u32[]{:S(2)}) collective-permute-start(bf16[32,1024]{1,0:T(8,128)(2,1)S(1)} %get-tuple-element.29), channel_id=1, source_target_pairs={{0,12},{4,8},{8,4},{12,0},{1,13},{5,9},{9,5},{13,1},{2,14},{6,10},... | collective-permute-start | bytes 196616 | tf_op jit(solution)/shard_map/ppermute | solution.py:214
  21.5 3.4 %collective-permute-start.7 = (bf16[32,1024]{1,0:T(8,128)(2,1)S(1)}, bf16[32,1024]{1,0:T(8,128)(2,1)S(1)}, u32[]{:S(2)}, u32[]{:S(2)}) collective-permute-start(bf16[32,1024]{1,0:T(8,128)(2,1)S(1)} %get-tuple-element.30), channel_id=1, source_target_pairs={{0,4},{4,0},{8,12},{12,8},{1,5},{5,1},{9,13},{13,9},{2,6},{6,2},{1... | collective-permute-start | bytes 196616 | tf_op jit(solution)/shard_map/ppermute | solution.py:214

commit v5 on v4

--- a/solution.py
+++ b/solution.py
@@ -32,22 +32,23 @@
     return pltpu.with_memory_space_constraint(value, pltpu.VMEM)
 
 
+def in_smem(value):
+    return pltpu.with_memory_space_constraint(value, pltpu.SMEM)
+
+
 def in_hbm(value):
     return pltpu.with_memory_space_constraint(value, pltpu.HBM)
 
 
-def prepare_kernel(starts, up, slots, edge_up, smem_starts, sems, *, count):
-    copies = [pltpu.make_async_copy(starts, smem_starts, sems.at[2])]
-    for side, first in enumerate((0, count - EDGE)):
-        copies.append(pltpu.make_async_copy(up.at[pl.ds(first, EDGE)], edge_up.at[side], sems.at[side]))
-    for copy in copies:
-        copy.start()
+def prepare_kernel(starts, slots, smem_starts, sem, *, count):
+    copy = pltpu.make_async_copy(starts, smem_starts, sem)
+    copy.start()
     first_block = lax.axis_index("weight") * count
     lanes = lax.broadcasted_iota(jnp.int32, slots.shape, 1)
     place = first_block + lax.broadcasted_iota(jnp.int32, slots.shape, 0) * 128 + lanes
     row = jnp.zeros(slots.shape, jnp.int32)
     first_row, enters, leaves = 0, 1, 1
-    copies[0].wait()
+    copy.wait()
     for f in range(1, smem_starts.shape[0]):
         start = smem_starts[f]
         row += (start <= place).astype(jnp.int32)
@@ -57,8 +58,6 @@
     enters = jnp.where(first_block == 0, 0, enters)
     flag_row = lax.broadcasted_iota(jnp.int32, slots.shape, 0) == slots.shape[0] - 1
     slots[...] = jnp.where(flag_row, jnp.where(lanes == 0, enters, leaves), row - first_row)
-    for copy in copies[1:]:
-        copy.wait()
 
 
 def slot_of(slots, block):
@@ -114,8 +113,15 @@
     lax.fori_loop(0, (groups[1] - groups[0]) // unroll, step, 0)
 
 
-def gate_kernel(slots, cols, gate, *refs, unroll):
-    pieces, (by_col, sums, whole) = refs[:-3], refs[-3:]
+def gate_kernel(slots, cols, gate, up, *refs, unroll):
+    pieces, (by_col, sums, edge_up, whole, sems) = refs[:-5], refs[-5:]
+    count = cols.shape[0]
+    copies = [
+        pltpu.make_async_copy(up.at[pl.ds(first, EDGE)], edge_up.at[side], sems.at[side])
+        for side, first in enumerate((0, count - EDGE))
+    ]
+    for copy in copies:
+        copy.start()
     col_blocks, rows = by_col.shape[0] - 1, by_col.shape[1]
     me = lax.axis_index("weight")
     for distance, piece in enumerate(pieces):
@@ -125,7 +131,9 @@
         by_col[c] = merged[:, c * 128 : (c + 1) * 128]
     by_col[col_blocks] = jnp.zeros((rows, 128), BF16)
     sums[...] = jnp.zeros_like(sums)
-    add_rows(slots, cols, by_col, gate, sums, (0, cols.shape[0] // GROUP), unroll)
+    add_rows(slots, cols, by_col, gate, sums, (0, count // GROUP), unroll)
+    for copy in copies:
+        copy.wait()
 
 
 def edge_kernel(slots, cols, by_col, edge_up, gate_sums, edge_sums, to_inner, to_outer):
@@ -217,33 +225,31 @@
     arrived = {distance: swap(tokens, distance) for distance in order}
     pieces = [tokens] + [arrived[distance] for distance in range(1, size)]
     slot_rows = -(-count // 128) + 1
-    slots, edge_up = pl.pallas_call(
+    slots = pl.pallas_call(
         functools.partial(prepare_kernel, count=count),
-        out_shape=(
-            jax.ShapeDtypeStruct((slot_rows, 128), jnp.int32),
-            pltpu.VMEM((2, EDGE, width, width), BF16),
-        ),
-        in_specs=[HB, HB],
-        out_specs=(VM, VM),
-        scratch_shapes=[pltpu.SMEM(row_starts.shape, jnp.int32), pltpu.SemaphoreType.DMA((3,))],
-        compiler_params=limit(4),
-        cost_estimate=cost(2**33),
+        out_shape=jax.ShapeDtypeStruct((slot_rows, 128), jnp.int32),
+        in_specs=[HB],
+        out_specs=VM,
+        scratch_shapes=[pltpu.SMEM(row_starts.shape, jnp.int32), pltpu.SemaphoreType.DMA(())],
+        compiler_params=limit(2),
+        cost_estimate=cost(2**36),
         name="prepare",
-    )(in_hbm(row_starts), in_hbm(up_blocks))
+    )(in_hbm(row_starts))
     unroll = largest_divisor(count // GROUP, 28)
-    by_col, gate_sums = pl.pallas_call(
+    by_col, gate_sums, edge_up = pl.pallas_call(
         functools.partial(gate_kernel, unroll=unroll),
         out_shape=(
             pltpu.VMEM((col_blocks + 1, rows, width), BF16),
             pltpu.VMEM((row_slots, rows, width), F32),
+            pltpu.VMEM((2, EDGE, width, width), BF16),
         ),
-        in_specs=[SM, SM] + [VM] * (size + 1),
-        out_specs=(VM, VM),
-        scratch_shapes=[pltpu.VMEM((size, slab, model_width), BF16)],
+        in_specs=[SM, SM, VM, HB] + [VM] * size,
+        out_specs=(VM, VM, VM),
+        scratch_shapes=[pltpu.VMEM((size, slab, model_width), BF16), pltpu.SemaphoreType.DMA((2,))],
         compiler_params=limit(8),
         cost_estimate=cost(2**20),
         name="gate",
-    )(slots, gate_cols, in_vmem(gate_blocks), *pieces)
+    )(in_smem(slots), in_smem(gate_cols), in_vmem(gate_blocks), in_hbm(up_blocks), *pieces)
     edge_sums, to_inner, to_outer = pl.pallas_call(
         edge_kernel,
         out_shape=(
@@ -256,7 +262,7 @@
         compiler_params=limit(4),
         cost_estimate=cost(2**20),
         name="edges",
-    )(slots, gate_cols, in_vmem(by_col), edge_up, in_vmem(gate_sums))
+    )(in_smem(slots), in_smem(gate_cols), in_vmem(by_col), in_vmem(edge_up), in_vmem(gate_sums))
     outer_pairs = [(d, (d + 1 if d % 2 else d - 1) % size) for d in range(size)]
     from_outer = lax.ppermute(to_outer, "weight", outer_pairs)
     from_inner = swap(to_inner, 1)
@@ -272,7 +278,7 @@
         compiler_params=limit(8),
         cost_estimate=cost(2**20),
         name="up",
-    )(slots, gate_cols, in_vmem(by_col), in_vmem(up_blocks), in_vmem(edge_sums), in_vmem(gate_sums))
+    )(in_smem(slots), in_smem(gate_cols), in_vmem(by_col), in_vmem(up_blocks), in_vmem(edge_sums), in_vmem(gate_sums))
     outs = pl.pallas_call(
         functools.partial(down_kernel, unroll=unroll),
         out_shape=tuple(
@@ -288,7 +294,7 @@
         compiler_params=limit(8),
         cost_estimate=cost(2**20),
         name="down",
-    )(slots, down_cols, in_vmem(hidden), in_vmem(edges), from_inner, from_outer, in_vmem(down_blocks))
+    )(in_smem(slots), in_smem(down_cols), in_vmem(hidden), in_vmem(edges), from_inner, from_outer, in_vmem(down_blocks))
     received = {distance: swap(outs[distance], distance) for distance in order}
     total = outs[0]
     for distance in order:

time: 25.8 us -> 25.7 us (level)
  waiting for transfers between devices: 4.27 us -> 5.89 us
  Pallas kernels: 13.2 us -> 12.1 us
  starting transfers between devices: 7.23 us -> 6.75 us
    ppermute x7, waiting for transfers between devices: 4.27 us -> 5.89 us  [swap(): lax.ppermute(value, 'weight', [(d, d ^ distance) for d in range(size)])]
    pallas_call x1, Pallas kernels: 2.18 us -> 1.08 us  [per_device(): pl.pallas_call(functools.partial(prepare_kernel, count=count), out_shape=...]
    ppermute x1, starting transfers between devices: 1.27 us -> 0.78 us  [per_device(): from_outer = lax.ppermute(to_outer, 'weight', outer_pairs)]
  transfers between devices with their start and end apart: 8 -> 8, of which waited for: 3 -> 4; matrix products, arithmetic and copies ran while one was open for 0% -> 0% of each run, Pallas kernels for 21% -> 17%
where the time goes in v5:
time: 25.7 us; the launch traced here: 25.6 us
  Pallas kernels  12.1 us (47%)
  starting transfers between devices  6.75 us (26%)
  waiting for transfers between devices  5.89 us (23%)
  other arithmetic  0.67 us (3%)
    ppermute x7, starting transfers between devices, swap(): lax.ppermute(value, 'weight', [(d, d ^ distance) for d in range(size)])  5.97 us
    ppermute x7, waiting for transfers between devices, swap(): lax.ppermute(value, 'weight', [(d, d ^ distance) for d in range(size)])  5.89 us
    pallas_call x1, Pallas kernels, per_device(): pl.pallas_call(functools.partial(gate_kernel, unroll=unroll), out_shape=(...  3.52 us
    pallas_call x1, Pallas kernels, per_device(): pl.pallas_call(functools.partial(up_kernel, unroll=largest_divisor((count...  3.3 us
    pallas_call x1, Pallas kernels, per_device(): pl.pallas_call(functools.partial(down_kernel, unroll=unroll), out_shape=t...  3.11 us
    pallas_call x1, Pallas kernels, per_device(): pl.pallas_call(functools.partial(prepare_kernel, count=count), out_shape=...  1.08 us
    pallas_call x1, Pallas kernels, per_device(): pl.pallas_call(edge_kernel, out_shape=(pltpu.VMEM((2, EDGE // GROUP, 2 *...  1.06 us
    ppermute x1, starting transfers between devices, per_device(): from_outer = lax.ppermute(to_outer, 'weight', outer_pairs)  0.78 us
  transfers between devices with their start and end apart: 8, of which 4 were waited for; matrix products, arithmetic and copies ran while one was open for 0% of the time, Pallas kernels for 17%

profile of v5, /device:TPU:0, one launch (start us, length us, event | category | flops | bytes accessed | tf_op | source)
XLA Modules:
  0.0 25.6 jit_solution(11931356923230973795)
XLA Ops:
  0.0 0.0 copy-start.2
  0.0 0.0 copy-start.3
  0.0 0.0 copy-start.1
  0.0 3.0 %collective-permute-start.1 = (bf16[1,8,4096]{2,1,0:T(8,128)(2,1)}, bf16[1,8,4096]{2,1,0:T(8,128)(2,1)S(1)}, u32[]{:S(2)}, u32[]{:S(2)}) collective-permute-start(bf16[1,8,4096]{2,1,0:T(8,128)(2,1)} %refs_0_.1), channel_id=1, source_target_pairs={{0,8},{4,12},{8,0},{12,4},{1,9},{5,13},{9,1},{13,5},{2,10},{6,14},... | collective-permute-start | bytes 196616 | tf_op jit(solution)/shard_map/ppermute | solution.py:222
  3.0 0.0 collective-permute-start
  3.0 0.2 collective-permute-start.2
  3.2 1.1 %prepare.1.slots = s32[5,128]{1,0:T(8,128)S(1)} custom-call(s32[113]{0:T(128)} %starts.1), custom_call_target="tpu_custom_call" | custom-call | flops 68719476736 | bytes 1024 | tf_op jit(solution)/shard_map/prepare/pallas_call | solution.py:228
  4.3 0.0 copy-start
  4.3 1.3 %collective-permute-done.1.refs_2_ = bf16[1,8,4096]{2,1,0:T(8,128)(2,1)S(1)} collective-permute-done((bf16[1,8,4096]{2,1,0:T(8,128)(2,1)}, bf16[1,8,4096]{2,1,0:T(8,128)(2,1)S(1)}, u32[]{:S(2)}, u32[]{:S(2)}) %collective-permute-start.1) | collective-permute-done | bytes 65568 | tf_op jit(solution)/shard_map/ppermute | solution.py:222
  5.6 0.0 collective-permute-done.refs_1_
  5.6 1.3 %collective-permute-done.2.refs_3_ = bf16[1,8,4096]{2,1,0:T(8,128)(2,1)S(1)} collective-permute-done((bf16[1,8,4096]{2,1,0:T(8,128)(2,1)}, bf16[1,8,4096]{2,1,0:T(8,128)(2,1)S(1)}, u32[]{:S(2)}, u32[]{:S(2)}) %collective-permute-start.2) | collective-permute-done | bytes 65568 | tf_op jit(solution)/shard_map/ppermute | solution.py:222
  7.0 0.0 copy-done.2
  7.0 0.0 copy-done.3
  7.0 0.0 copy-done.1
  7.0 0.0 slice-start
  7.0 0.0 slice-start.1
  7.0 0.0 slice-start.2
  7.0 3.5 %gate.2 = (bf16[33,32,128]{2,1,0:T(8,128)(2,1)S(1)}, f32[58,32,128]{2,1,0:T(8,128)S(1)}, bf16[2,24,128,128]{3,2,1,0:T(8,128)(2,1)S(1)}) custom-call(s32[5,128]{1,0:T(8,128)S(1)} %prepare.1.slots, s32[448]{0:T(512)S(1)} %copy-done.3, bf16[448,128,128]{2,1,0:T(8,128)(2,1)S(1)} %copy-done.1, bf16[448,128,128]{2,1,0:T(8,128)(2,1)} %up.5, ...), custom_call_target="tpu_custom_call" | custom-call | flops 1048576 | bytes 1024 | tf_op jit(solution)/shard_map/gate/pallas_call | solution.py:239
  10.5 0.0 copy-start.4
  10.6 1.1 %edges.1 = (f32[2,3,64,128]{3,2,1,0:T(8,128)S(1)}, bf16[32,256]{1,0:T(8,128)(2,1)S(1)}, bf16[32,256]{1,0:T(8,128)(2,1)S(1)}) custom-call(s32[5,128]{1,0:T(8,128)S(1)} %prepare.1.slots, s32[448]{0:T(512)S(1)} %copy-done.3, bf16[33,32,128]{2,1,0:T(8,128)(2,1)S(1)} %get-tuple-element.17.by_col, bf16[2,24,128,128]{3,2,1,0:T(8,128)(2,1)S(1)} %get-tuple-element.18.edge_up, ...), custom_call_target="tpu_custom_call" | custom-call | flops 1048576 | bytes 1024 | tf_op jit(solution)/shard_map/edges/pallas_call | solution.py:253
  11.6 0.6 %collective-permute-start.3 = (bf16[32,256]{1,0:T(8,128)(2,1)S(1)}, bf16[32,256]{1,0:T(8,128)(2,1)S(1)}, u32[]{:S(2)}, u32[]{:S(2)}) collective-permute-start(bf16[32,256]{1,0:T(8,128)(2,1)S(1)} %get-tuple-element.23), channel_id=1, source_target_pairs={{0,4},{4,0},{8,12},{12,8},{1,5},{5,1},{9,13},{13,9},{2,6},{6,2},{1... | collective-permute-start | bytes 49160 | tf_op jit(solution)/shard_map/ppermute | solution.py:222
  12.2 0.8 %collective-permute-start.4 = (bf16[32,256]{1,0:T(8,128)(2,1)S(1)}, bf16[32,256]{1,0:T(8,128)(2,1)S(1)}, u32[]{:S(2)}, u32[]{:S(2)}) collective-permute-start(bf16[32,256]{1,0:T(8,128)(2,1)S(1)} %get-tuple-element.24), channel_id=1, source_target_pairs={{0,12},{4,8},{8,4},{12,0},{1,13},{5,9},{9,5},{13,1},{2,14},{6,10},... | collective-permute-start | bytes 49160 | tf_op jit(solution)/shard_map/ppermute | solution.py:267
  13.0 0.0 copy-done
  13.0 0.0 slice-start.3
  13.0 3.3 %up.4 = (bf16[58,32,128]{2,1,0:T(8,128)(2,1)S(1)}, f32[2,2,32,128]{3,2,1,0:T(8,128)S(1)}) custom-call(s32[5,128]{1,0:T(8,128)S(1)} %prepare.1.slots, s32[448]{0:T(512)S(1)} %copy-done.3, bf16[33,32,128]{2,1,0:T(8,128)(2,1)S(1)} %get-tuple-element.17.by_col, bf16[448,128,128]{2,1,0:T(8,128)(2,1)S(1)} %copy-done, ...), custom_call_target="tpu_custom_call" | custom-call | flops 1048576 | bytes 1024 | tf_op jit(solution)/shard_map/up/pallas_call | solution.py:269
  16.3 0.0 collective-permute-done.3.from_inner
  16.3 0.0 collective-permute-done.4.from_outer
  16.3 0.0 slice-done
  16.3 0.0 slice-done.1
  16.3 0.0 slice-done.2
  16.3 0.0 copy-done.4
  16.3 0.0 slice-done.3
  16.3 3.1 %down.2 = (f32[32,1024]{1,0:T(8,128)S(1)}, bf16[32,1024]{1,0:T(8,128)(2,1)S(1)}, bf16[32,1024]{1,0:T(8,128)(2,1)S(1)}, bf16[32,1024]{1,0:T(8,128)(2,1)S(1)}) custom-call(s32[5,128]{1,0:T(8,128)S(1)} %prepare.1.slots, s32[448]{0:T(512)S(1)} %copy-done.4, bf16[58,32,128]{2,1,0:T(8,128)(2,1)S(1)} %get-tuple-element.21.hidden, ...), custom_call_target="tpu_custom_call" | custom-call | flops 1048576 | bytes 1024 | tf_op jit(solution)/shard_map/down/pallas_call | solution.py:282
  19.5 1.0 %collective-permute-start.5 = (bf16[32,1024]{1,0:T(8,128)(2,1)S(1)}, bf16[32,1024]{1,0:T(8,128)(2,1)S(1)}, u32[]{:S(2)}, u32[]{:S(2)}) collective-permute-start(bf16[32,1024]{1,0:T(8,128)(2,1)S(1)} %get-tuple-element.26), channel_id=1, source_target_pairs={{0,8},{4,12},{8,0},{12,4},{1,9},{5,13},{9,1},{13,5},{2,10},{6,14},... | collective-permute-start | bytes 196616 | tf_op jit(solution)/shard_map/ppermute | solution.py:222
  20.5 0.9 %collective-permute-start.6 = (bf16[32,1024]{1,0:T(8,128)(2,1)S(1)}, bf16[32,1024]{1,0:T(8,128)(2,1)S(1)}, u32[]{:S(2)}, u32[]{:S(2)}) collective-permute-start(bf16[32,1024]{1,0:T(8,128)(2,1)S(1)} %get-tuple-element.27), channel_id=1, source_target_pairs={{0,12},{4,8},{8,4},{12,0},{1,13},{5,9},{9,5},{13,1},{2,14},{6,10},... | collective-permute-start | bytes 196616 | tf_op jit(solution)/shard_map/ppermute | solution.py:222
  21.3 0.3 %collective-permute-start.7 = (bf16[32,1024]{1,0:T(8,128)(2,1)S(1)}, bf16[32,1024]{1,0:T(8,128)(2,1)S(1)}, u32[]{:S(2)}, u32[]{:S(2)}) collective-permute-start(bf16[32,1024]{1,0:T(8,128)(2,1)S(1)} %get-tuple-element.28), channel_id=1, source_target_pairs={{0,4},{4,0},{8,12},{12,8},{1,5},{5,1},{9,13},{13,9},{2,6},{6,2},{1... | collective-permute-start | bytes 196616 | tf_op jit(solution)/shard_map/ppermute | solution.py:222
  21.7 2.8 %collective-permute-done.5 = bf16[32,1024]{1,0:T(8,128)(2,1)S(1)} collective-permute-done((bf16[32,1024]{1,0:T(8,128)(2,1)S(1)}, bf16[32,1024]{1,0:T(8,128)(2,1)S(1)}, u32[]{:S(2)}, u32[]{:S(2)}) %collective-permute-start.5) | collective-permute-done | bytes 65568 | tf_op jit(solution)/shard_map/ppermute | solution.py:222
  24.4 0.5 %collective-permute-done.6 = bf16[32,1024]{1,0:T(8,128)(2,1)S(1)} collective-permute-done((bf16[32,1024]{1,0:T(8,128)(2,1)S(1)}, bf16[32,1024]{1,0:T(8,128)(2,1)S(1)}, u32[]{:S(2)}, u32[]{:S(2)}) %collective-permute-start.6) | collective-permute-done | bytes 65568 | tf_op jit(solution)/shard_map/ppermute | solution.py:222
  24.9 0.0 collective-permute-done.7
  24.9 0.7 %fusion = bf16[4,8,1024]{2,1,0:T(8,128)(2,1)} fusion(bf16[32,1024]{1,0:T(8,128)(2,1)S(1)} %collective-permute-done.7, bf16[32,1024]{1,0:T(8,128)(2,1)S(1)} %collective-permute-done.6, f32[32,1024]{1,0:T(8,128)S(1)} %get-tuple-element.25, bf16[32,1024]{1,0:T(8,128)(2,1)S(1)} %collective-permute-done.5), kind=kLoop, calls=%fused_computation.1 | loop fusion | flops 229376 | bytes 393216 | tf_op jit(solution)/shard_map/reshape | solution.py:302
  (1 shorter events, 0.0 us)
Async XLA Ops:
  0.0 7.0 %copy-start.2 = (bf16[1,8,4096]{2,1,0:T(8,128)(2,1)S(1)}, bf16[1,8,4096]{2,1,0:T(8,128)(2,1)}, u32[]{:S(2)}) copy-start(bf16[1,8,4096]{2,1,0:T(8,128)(2,1)} %refs_0_.1) | copy-start | bytes 196612
  0.0 7.0 %copy-start.3 = (s32[448]{0:T(512)S(1)}, s32[448]{0:T(512)}, u32[]{:S(2)}) copy-start(s32[448]{0:T(512)} %cols.6) | copy-start | bytes 5380
  0.0 7.0 %copy-start.1 = (bf16[448,128,128]{2,1,0:T(8,128)(2,1)S(1)}, bf16[448,128,128]{2,1,0:T(8,128)(2,1)}, u32[]{:S(2)}) copy-start(bf16[448,128,128]{2,1,0:T(8,128)(2,1)} %gate.3) | copy-start | bytes 44040196
  0.0 5.6 %collective-permute-start.1 = (bf16[1,8,4096]{2,1,0:T(8,128)(2,1)}, bf16[1,8,4096]{2,1,0:T(8,128)(2,1)S(1)}, u32[]{:S(2)}, u32[]{:S(2)}) collective-permute-start(bf16[1,8,4096]{2,1,0:T(8,128)(2,1)} %refs_0_.1), channel_id=1, source_target_pairs={{0,8},{4,12},{8,0},{12,4},{1,9},{5,13},{9,1},{13,5},{2,10},{6,14},... | collective-permute-start | bytes 196616 | tf_op jit(solution)/shard_map/ppermute | solution.py:222
  3.0 2.6 %collective-permute-start = (bf16[1,8,4096]{2,1,0:T(8,128)(2,1)}, bf16[1,8,4096]{2,1,0:T(8,128)(2,1)S(1)}, u32[]{:S(2)}, u32[]{:S(2)}) collective-permute-start(bf16[1,8,4096]{2,1,0:T(8,128)(2,1)} %refs_0_.1), channel_id=1, source_target_pairs={{0,4},{4,0},{8,12},{12,8},{1,5},{5,1},{9,13},{13,9},{2,6},{6,2},{1... | collective-permute-start | bytes 196616 | tf_op jit(solution)/shard_map/ppermute | solution.py:222
  3.0 4.0 %collective-permute-start.2 = (bf16[1,8,4096]{2,1,0:T(8,128)(2,1)}, bf16[1,8,4096]{2,1,0:T(8,128)(2,1)S(1)}, u32[]{:S(2)}, u32[]{:S(2)}) collective-permute-start(bf16[1,8,4096]{2,1,0:T(8,128)(2,1)} %refs_0_.1), channel_id=1, source_target_pairs={{0,12},{4,8},{8,4},{12,0},{1,13},{5,9},{9,5},{13,1},{2,14},{6,10},... | collective-permute-start | bytes 196616 | tf_op jit(solution)/shard_map/ppermute | solution.py:222
  4.3 8.6 %copy-start = (bf16[448,128,128]{2,1,0:T(8,128)(2,1)S(1)}, bf16[448,128,128]{2,1,0:T(8,128)(2,1)}, u32[]{:S(2)}) copy-start(bf16[448,128,128]{2,1,0:T(8,128)(2,1)} %up.5) | copy-start | bytes 44040196
  7.0 9.3 %slice-start = ((s8[14680064]{0:T(1024)(128)(4,1)}), s8[4194304]{0:T(1024)(128)(4,1)S(1)}, s32[]{:S(2)}) async-start(s8[14680064]{0:T(1024)(128)(4,1)} %bitcast.2), calls=%async_computation | async-start | bytes 8388608
  7.0 9.3 %slice-start.1 = ((s8[14680064]{0:T(1024)(128)(4,1)}), s8[4194304]{0:T(1024)(128)(4,1)S(1)}, s32[]{:S(2)}) async-start(s8[14680064]{0:T(1024)(128)(4,1)} %bitcast.2), calls=%async_computation.1 | async-start | bytes 8388608
  7.0 9.3 %slice-start.2 = ((s8[14680064]{0:T(1024)(128)(4,1)}), s8[4194304]{0:T(1024)(128)(4,1)S(1)}, s32[]{:S(2)}) async-start(s8[14680064]{0:T(1024)(128)(4,1)} %bitcast.2), calls=%async_computation.2 | async-start | bytes 8388608
  10.5 5.8 %copy-start.4 = (s32[448]{0:T(512)S(1)}, s32[448]{0:T(512)}, u32[]{:S(2)}) copy-start(s32[448]{0:T(512)} %cols.7) | copy-start | bytes 5380
  11.6 4.7 %collective-permute-start.3 = (bf16[32,256]{1,0:T(8,128)(2,1)S(1)}, bf16[32,256]{1,0:T(8,128)(2,1)S(1)}, u32[]{:S(2)}, u32[]{:S(2)}) collective-permute-start(bf16[32,256]{1,0:T(8,128)(2,1)S(1)} %get-tuple-element.23), channel_id=1, source_target_pairs={{0,4},{4,0},{8,12},{12,8},{1,5},{5,1},{9,13},{13,9},{2,6},{6,2},{1... | collective-permute-start | bytes 49160 | tf_op jit(solution)/shard_map/ppermute | solution.py:222
  12.2 4.1 %collective-permute-start.4 = (bf16[32,256]{1,0:T(8,128)(2,1)S(1)}, bf16[32,256]{1,0:T(8,128)(2,1)S(1)}, u32[]{:S(2)}, u32[]{:S(2)}) collective-permute-start(bf16[32,256]{1,0:T(8,128)(2,1)S(1)} %get-tuple-element.24), channel_id=1, source_target_pairs={{0,12},{4,8},{8,4},{12,0},{1,13},{5,9},{9,5},{13,1},{2,14},{6,10},... | collective-permute-start | bytes 49160 | tf_op jit(solution)/shard_map/ppermute | solution.py:267
  13.0 3.4 %slice-start.3 = ((s8[14680064]{0:T(1024)(128)(4,1)}), s8[2097152]{0:T(1024)(128)(4,1)S(1)}, s32[]{:S(2)}) async-start(s8[14680064]{0:T(1024)(128)(4,1)} %bitcast.2), calls=%async_computation.3 | async-start | bytes 4194304
  19.5 5.0 %collective-permute-start.5 = (bf16[32,1024]{1,0:T(8,128)(2,1)S(1)}, bf16[32,1024]{1,0:T(8,128)(2,1)S(1)}, u32[]{:S(2)}, u32[]{:S(2)}) collective-permute-start(bf16[32,1024]{1,0:T(8,128)(2,1)S(1)} %get-tuple-element.26), channel_id=1, source_target_pairs={{0,8},{4,12},{8,0},{12,4},{1,9},{5,13},{9,1},{13,5},{2,10},{6,14},... | collective-permute-start | bytes 196616 | tf_op jit(solution)/shard_map/ppermute | solution.py:222
  20.5 4.4 %collective-permute-start.6 = (bf16[32,1024]{1,0:T(8,128)(2,1)S(1)}, bf16[32,1024]{1,0:T(8,128)(2,1)S(1)}, u32[]{:S(2)}, u32[]{:S(2)}) collective-permute-start(bf16[32,1024]{1,0:T(8,128)(2,1)S(1)} %get-tuple-element.27), channel_id=1, source_target_pairs={{0,12},{4,8},{8,4},{12,0},{1,13},{5,9},{9,5},{13,1},{2,14},{6,10},... | collective-permute-start | bytes 196616 | tf_op jit(solution)/shard_map/ppermute | solution.py:222
  21.3 3.6 %collective-permute-start.7 = (bf16[32,1024]{1,0:T(8,128)(2,1)S(1)}, bf16[32,1024]{1,0:T(8,128)(2,1)S(1)}, u32[]{:S(2)}, u32[]{:S(2)}) collective-permute-start(bf16[32,1024]{1,0:T(8,128)(2,1)S(1)} %get-tuple-element.28), channel_id=1, source_target_pairs={{0,4},{4,0},{8,12},{12,8},{1,5},{5,1},{9,13},{13,9},{2,6},{6,2},{1... | collective-permute-start | bytes 196616 | tf_op jit(solution)/shard_map/ppermute | solution.py:222
